TPU v7x, 32 devices: a whole 2x2x4 slice. The times are simulated.
32 devices in a mesh: occ: 8 (over z, x), vir: 4 (over y, core).
Axes of the slice: x: 2, y: 2, z: 4, core: 2. Of those that a mesh axis runs over, the one named last changes fastest.
Arguments:
- amps: float32 [1024, 4, 1024], P('occ', 'vir'), may hold values from -6 to 6
- resid: float32 [1024, 4, 1024], P('occ', 'vir'), may hold values from -6 to 6
- ints: float32 [4, 1024, 1024], P('vir', 'occ'), may hold values from -0.5 to 0.5
- tasks: int32 [4], replicated, may hold values from 0 to 3
- pair_tiles: int32 [4, 2], replicated, may hold values from 0 to 18
- irreps: int32 [19, 32], replicated, may hold values from 0 to 7
Outputs:
- updated: float32 [1024, 4, 1024], P('occ', 'vir')
All inputs are finite; a program needn't handle non-finite values.
Results may differ from a plain program's by a relative error of at most 0.0003.
Values sent between devices are 32-bit elements; how exact they have to be, the bound alone decides.
No kernel may reach another device: no remote copies, remote signals or barrier semaphores. Data moves between devices by JAX's collectives and lax.ppermute only.
A program may use at most 64 MiB of HBM per device.

v0:
```python
import jax
import jax.numpy as jnp
from jax import lax
from jax.sharding import PartitionSpec as P


def tile_irreps(tile_pair, irreps):
    tile_count = irreps.shape[0]
    tile_ids = jnp.arange(tile_count, dtype=jnp.int32)
    first_row = jnp.sum(jnp.where(tile_ids[:, None] == tile_pair[0], irreps, 0), axis=0)
    second_row = jnp.sum(jnp.where(tile_ids[:, None] == tile_pair[1], irreps, 0), axis=0)
    return jnp.bitwise_xor(first_row[:, None], second_row[None, :]).reshape(-1)


def contract(left, right):
    return lax.dot_general(
        left,
        right,
        (((1,), (1,)), ((), ())),
        precision=lax.Precision.HIGHEST,
        preferred_element_type=jnp.float32,
    )


def shards(amps, resid, ints, tasks, pair_tiles, irreps):
    own_tile = lax.axis_index("vir")
    cd_tile = lax.dynamic_index_in_dim(tasks, own_tile, 0, keepdims=False)
    ab_irrep = tile_irreps(
        lax.dynamic_index_in_dim(pair_tiles, own_tile, 0, keepdims=False), irreps
    )
    cd_irrep = tile_irreps(lax.dynamic_index_in_dim(pair_tiles, cd_tile, 0, keepdims=False), irreps)
    spread = lax.all_to_all(amps, "vir", split_axis=0, concat_axis=1, tiled=True)
    picked = jnp.take(spread, tasks, axis=1)
    returned = lax.all_to_all(picked, "vir", split_axis=1, concat_axis=0, tiled=True)
    chosen = returned[:, 0, :]
    effective = jnp.where(
        ab_irrep[:, None] == cd_irrep[None, :],
        lax.all_gather(ints, "occ", axis=1, tiled=True)[0],
        0.0,
    )
    ladder = contract(chosen, effective)
    return resid + ladder[:, None, :]


def solution(mesh):
    in_specs = (P("occ", "vir", None), P("occ", "vir", None), P("vir", "occ", None), P(), P(), P())
    out_specs = P("occ", "vir", None)
    return jax.shard_map(shards, mesh=mesh, in_specs=in_specs, out_specs=out_specs, check_vma=False)
```

profile of v0, /device:TPU:0, one launch (start us, length us, event | category | flops | bytes accessed | tf_op | source)
XLA Modules:
  0.0 100.4 jit_solution(7575202591109431762)
XLA Ops:
  6.5 0.0 copy-start
  6.5 0.0 all-gather.2.cloned.1.call-start
  6.5 0.7 all-gather.2.cloned.1.call-update
  7.3 4.2 %all-to-all-start = ((f32[128,1,1024]{2,1,0:T(1,128)}), f32[128,1,1024]{2,1,0:T(1,128)S(1)}, u32[]{:S(2)}, u32[]{:S(2)}) async-start(f32[128,1,1024]{2,1,0:T(1,128)} %param.6), calls=%async_computation | async-start | bytes 1048576 | tf_op jit(solution)/shard_map/all_to_all | solution.py:32
  11.5 1.2 %dynamic_slice.12 = s32[1]{0:T(128)} dynamic-slice(s32[4]{0:T(128)} %param.9, s32[]{:T(128)S(6)} %select_n.40), dynamic_slice_sizes={1} | dynamic-slice | bytes 12 | tf_op jit(solution)/shard_map/jit(dynamic_index_in_dim)/dynamic_slice | solution.py:27
  14.7 0.8 constant_dynamic-slice_fusion
  15.5 0.6 fusion.14
  16.1 0.6 iota_compare_fusion
  16.8 0.7 iota_compare_fusion.1
  17.4 0.7 iota_compare_fusion.2
  18.1 0.7 compare_select_fusion
  18.8 0.6 iota_compare_fusion.3
  19.4 0.8 select_reduce_fusion.3
  20.2 0.7 compare_and_fusion
  20.9 0.0 all-to-all-done
  20.9 0.1 copy.12
  21.0 0.6 gather_fusion
  21.6 0.9 select_bitcast_fusion
  22.5 3.5 %all-to-all-start.1 = ((f32[32,4,1024]{2,0,1:T(8,128)}), f32[32,4,1024]{2,0,1:T(8,128)S(1)}, u32[]{:S(2)}, u32[]{:S(2)}) async-start(f32[32,4,1024]{2,0,1:T(8,128)} %select_bitcast_fusion), calls=%async_computation.1 | async-start | bytes 1048576 | tf_op jit(solution)/shard_map/all_to_all | solution.py:34
  26.0 0.1 broadcast_xor_fusion.1
  26.0 0.1 xor.43
  26.1 0.1 broadcast_xor_fusion
  26.2 0.1 xor.47
  26.3 8.6 %all-to-all-done.1 = f32[32,4,1024]{2,0,1:T(8,128)S(1)} async-done(((f32[32,4,1024]{2,0,1:T(8,128)}), f32[32,4,1024]{2,0,1:T(8,128)S(1)}, u32[]{:S(2)}, u32[]{:S(2)}) %all-to-all-start.1) | async-done | bytes 524320 | tf_op jit(solution)/shard_map/all_to_all | solution.py:34
  34.8 50.8 %all-gather.2.cloned.1.call-done = f32[1,1024,1024]{2,1,0:T(8,128)} async-done(((f32[1,128,1024]{2,1,0:T(8,128)}), f32[1,1024,1024]{2,1,0:T(8,128)}) %all-gather.2.cloned.1.call-update) | async-done | bytes 4194320 | tf_op jit(solution)/shard_map/all_gather | solution.py:38
  85.6 0.0 copy-done
  85.6 6.6 %fusion.10 = f32[128,1,1024]{2,0,1:T(8,128)S(1)} fusion(f32[128,1024]{1,0:T(8,128)S(1)} %bitcast.32, f32[1,1024,1024]{2,1,0:T(8,128)} %all-gather.2.cloned.1.call-done, s32[1024]{0:T(1024)S(1)} %xor.47, s32[1024]{0:T(1024)S(1)} %xor.43, f32[128,1,1024]{2,1,0:T(1,128)S(1)} %copy-done), kind=kOutput, calls=%fused_computation.9 | convolution fusion | flops 1612840960 | bytes 5775360 | tf_op jit(solution)/shard_map/dot_general | solution.py:16
  92.3 1.3 %copy.8 = f32[128,1,1024]{2,1,0:T(1,128)} copy(f32[128,1,1024]{2,0,1:T(8,128)S(1)} %fusion.10) | data formatting | bytes 1048576 | tf_op jit(solution)/shard_map/add | solution.py:42
  (1 shorter events, 0.0 us)
Async XLA Ops:
  6.5 79.1 %copy-start = (f32[128,1,1024]{2,1,0:T(1,128)S(1)}, f32[128,1,1024]{2,1,0:T(1,128)}, u32[]{:S(2)}) copy-start(f32[128,1,1024]{2,1,0:T(1,128)} %param.7) | copy-start | bytes 1572868
  6.5 79.1 %all-gather.2.cloned.1.call-start = ((), (), s32[]{:S(2)}) async-start(), calls=%async_computation.2 | async-start | bytes 4718592 | tf_op jit(solution)/shard_map/all_gather | solution.py:38
  7.3 13.6 %all-to-all-start = ((f32[128,1,1024]{2,1,0:T(1,128)}), f32[128,1,1024]{2,1,0:T(1,128)S(1)}, u32[]{:S(2)}, u32[]{:S(2)}) async-start(f32[128,1,1024]{2,1,0:T(1,128)} %param.6), calls=%async_computation | async-start | bytes 1048576 | tf_op jit(solution)/shard_map/all_to_all | solution.py:32
  22.5 12.3 %all-to-all-start.1 = ((f32[32,4,1024]{2,0,1:T(8,128)}), f32[32,4,1024]{2,0,1:T(8,128)S(1)}, u32[]{:S(2)}, u32[]{:S(2)}) async-start(f32[32,4,1024]{2,0,1:T(8,128)} %select_bitcast_fusion), calls=%async_computation.1 | async-start | bytes 1048576 | tf_op jit(solution)/shard_map/all_to_all | solution.py:34
Sparse Core Ops, SparseCore 0:
  9.5 76.0 all-gather.1
where the time goes:
time: 101 us; the launch traced here: 100 us
  waiting for transfers between devices  60.1 us (60%)
  between operations  15.4 us (15%)
  starting transfers between devices  7.73 us (8%)
  matrix products  6.62 us (7%)
  other arithmetic  5.77 us (6%)
  local copies, waits for them, and re-layouts  4.84 us (5%)
    all_gather x1, waiting for transfers between devices, shards(): lax.all_gather(ints, 'occ', axis=1, tiled=True)[0]  50.8 us
    all_to_all x1, waiting for transfers between devices, shards(): lax.all_to_all(picked, 'vir', split_axis=1, concat_axis=0, tiled=True)  8.56 us
    dot_general x1, matrix products, contract(): lax.dot_general(left, right, (((1,), (1,)), ((), ())), precision=lax.Prec...  6.62 us
    all_to_all x1, starting transfers between devices, shards(): lax.all_to_all(amps, 'vir', split_axis=0, concat_axis=1, tiled=True)  4.25 us
    all_to_all x1, starting transfers between devices, shards(): lax.all_to_all(picked, 'vir', split_axis=1, concat_axis=0, tiled=True)  3.48 us
  transfers between devices with their start and end apart: 3, of which 2 were waited for; matrix products, arithmetic and copies ran while one was open for 9% of the time, Pallas kernels for 0%

commit v1 on v0

v1 whole, which is shorter than its diff:
```python
import functools

import jax
import jax.numpy as jnp
from jax import lax
from jax.experimental import pallas as pl
from jax.experimental.pallas import tpu as pltpu
from jax.sharding import PartitionSpec as P

GROUP = 8
LANES = 128
DEPTH = 192

NT = (((1,), (1,)), ((), ()))
NN = (((1,), (0,)), ((), ()))


def dot(left, right, dims):
    return lax.dot_general(left, right, dims, preferred_element_type=jnp.float32)


def split(values):
    high = values.astype(jnp.bfloat16)
    return high, (values - high.astype(jnp.float32)).astype(jnp.bfloat16)


def iota(shape, dim):
    return lax.broadcasted_iota(jnp.int32, shape, dim)


def pair_rows(firsts, seconds, width):
    tile = firsts.shape[1]
    column, orbital = iota((tile, width), 1), iota((tile, width), 0)
    outer = (lax.div(column, tile) == orbital).astype(jnp.bfloat16)
    inner = (lax.rem(column, tile) == orbital).astype(jnp.bfloat16)
    spread = lambda rows, how: dot(rows.astype(jnp.float32).astype(jnp.bfloat16), how, NN).astype(jnp.int32)
    return jnp.bitwise_xor(spread(firsts, outer), spread(seconds, inner))


def ranks(irrep):
    width = irrep.shape[1]
    member = (irrep == iota(irrep.shape, 0)).astype(jnp.float32)
    parts = [member[:, at : at + LANES] for at in range(0, width, LANES)]
    before = (iota((LANES, LANES), 0) < iota((LANES, LANES), 1)).astype(jnp.bfloat16)
    inside = dot(jnp.concatenate(parts, axis=0).astype(jnp.bfloat16), before, NN)
    base = jnp.zeros((GROUP, 1), jnp.float32)
    out = []
    for place, part in enumerate(parts):
        count = inside[place * GROUP : (place + 1) * GROUP] + base
        out.append(jnp.sum(part * count, axis=0, keepdims=True))
        base = base + jnp.sum(part, axis=1, keepdims=True)
    return jnp.concatenate(out, axis=1).astype(jnp.int32)


def prep_kernel(depth, first_ref, tasks_ref, pairs_ref, irreps_ref, ints_ref, buf_ref, meta_ref):
    own, block = lax.axis_index("vir"), lax.axis_index("occ")
    height, width = ints_ref.shape
    tile = irreps_ref.shape[1]
    first = first_ref[0]
    cd = tasks_ref[own]
    row = lambda pair, side: irreps_ref[pl.ds(pairs_ref[pair, side], 1), :]
    wide = lambda values: jnp.broadcast_to(values, (GROUP, tile))
    ab_outer, ab_inner = row(own, 0), row(own, 1)
    irrep = pair_rows(
        jnp.concatenate([wide(row(cd, 0)), wide(ab_outer)], axis=0),
        jnp.concatenate([wide(row(cd, 1)), wide(ab_inner)], axis=0),
        width,
    )
    cd_irrep, ab_irrep = irrep[:GROUP], irrep[GROUP:]
    rank = ranks(cd_irrep) - first
    inside = jnp.logical_and(rank >= 0, rank < depth)
    slot = jnp.where(inside, cd_irrep[:1] * depth + rank, -1)
    meta_ref[...] = jnp.where(iota((GROUP, width), 0) == 0, jnp.broadcast_to(slot, (GROUP, width)), ab_irrep)
    pair = iota((height, tile), 0) + block * height
    lane = iota((height, tile), 1)
    outer = jnp.sum(jnp.where(lane == lax.div(pair, tile), ab_outer, 0), axis=1, keepdims=True)
    inner = jnp.sum(jnp.where(lane == lax.rem(pair, tile), ab_inner, 0), axis=1, keepdims=True)
    live = jnp.bitwise_xor(outer, inner) == cd_irrep[:1]
    high, low = split(jnp.where(live, ints_ref[...], 0.0))
    pick = (iota((depth, width), 0) == rank).astype(jnp.bfloat16)
    buf_ref[...] = dot(pick, high, NT) + dot(pick, low, NT)


def prep(first, tasks, pairs, irreps, ints, depth):
    height, width = ints.shape
    smem, vmem = pl.BlockSpec(memory_space=pltpu.SMEM), pl.BlockSpec(memory_space=pltpu.VMEM)
    return pl.pallas_call(
        functools.partial(prep_kernel, depth),
        out_shape=(
            jax.ShapeDtypeStruct((depth, height), jnp.float32),
            jax.ShapeDtypeStruct((GROUP, width), jnp.int32),
        ),
        in_specs=[smem, smem, smem, vmem, vmem],
        out_specs=(vmem, vmem),
        compiler_params=pltpu.CompilerParams(vmem_limit_bytes=32 << 20),
        cost_estimate=pl.CostEstimate(flops=4 * depth * height * width, bytes_accessed=4 * height * width, transcendentals=0),
        name="compact",
    )(first, tasks, pairs, irreps, ints)


def order_kernel(depth, count, *refs):
    tasks_ref, pairs_ref, irreps_ref, meta_ref = refs[:4]
    tiles, (out_ref, most_ref, held, sem) = refs[4 : 4 + count], refs[4 + count :]
    own = lax.axis_index("vir")
    chosen = jnp.bitwise_xor(tasks_ref[own], own)
    for number, tile_ref in enumerate(tiles):

        @pl.when(chosen == number)
        def _(tile_ref=tile_ref):
            copy = pltpu.make_async_copy(tile_ref.at[:, 0, :], held, sem)
            copy.start()
            copy.wait()

    width = meta_ref.shape[1]
    rows = lambda side: jnp.concatenate(
        [irreps_ref[pl.ds(pairs_ref[tasks_ref[k], side], 1), :] for k in range(tasks_ref.shape[0])], axis=0
    )
    irrep = pair_rows(rows(0), rows(1), width)
    most = jnp.zeros((irrep.shape[0], 1), jnp.int32)
    for g in range(GROUP):
        most = jnp.maximum(most, jnp.sum((irrep == g).astype(jnp.int32), axis=1, keepdims=True))
    most_ref[0] = jnp.max(most)

    high, low = split(held[...])
    both = jnp.concatenate([high, low], axis=0)
    for at in range(0, GROUP * depth, GROUP * depth // 4):
        size = GROUP * depth // 4
        place = (iota((size, width), 0) + at == meta_ref[:1]).astype(jnp.bfloat16)
        out_ref[:, at : at + size] = dot(both, place, NT).astype(jnp.bfloat16)


def order(tasks, pairs, irreps, meta, tiles, depth):
    height, _, width = tiles[0].shape
    smem, vmem = pl.BlockSpec(memory_space=pltpu.SMEM), pl.BlockSpec(memory_space=pltpu.VMEM)
    return pl.pallas_call(
        functools.partial(order_kernel, depth, len(tiles)),
        out_shape=(
            jax.ShapeDtypeStruct((2 * height, GROUP * depth), jnp.bfloat16),
            jax.ShapeDtypeStruct((1,), jnp.int32),
        ),
        in_specs=[smem, smem, vmem, vmem] + [pl.BlockSpec(memory_space=pl.ANY)] * len(tiles),
        out_specs=(vmem, smem),
        scratch_shapes=[pltpu.VMEM((height, width), jnp.float32), pltpu.SemaphoreType.DMA],
        compiler_params=pltpu.CompilerParams(vmem_limit_bytes=32 << 20),
        cost_estimate=pl.CostEstimate(
            flops=4 * height * width * GROUP * depth, bytes_accessed=4 * height * width, transcendentals=0
        ),
        name="order_amplitudes",
    )(tasks, pairs, irreps, meta, *tiles)


def ladder_kernel(depth, masks, meta_ref, amps_ref, *refs):
    count = len(masks)
    pieces, (base_ref, out_ref, held, sems) = refs[:count], refs[count:]
    block = lax.axis_index("occ")
    height = held.shape[0]
    size = pieces[0].shape[1]
    places = [pl.ds(pl.multiple_of(jnp.bitwise_xor(block, mask) * size, LANES), size) for mask in masks]
    loads = [
        pltpu.make_async_copy(base_ref.at[:, 0, place], held.at[:, n * size : (n + 1) * size], sems.at[n])
        for n, place in enumerate(places)
    ]
    for load in loads:
        load.start()
    high, low = split(jnp.concatenate([piece[...] for piece in pieces], axis=1))
    irrep = jnp.concatenate([meta_ref[1:2, place] for place in places], axis=1)
    zero = jnp.zeros((), jnp.bfloat16)
    blocks = lambda values: jnp.concatenate([jnp.where(irrep == g, values, zero) for g in range(GROUP)], axis=0)
    both = dot(amps_ref[...], blocks(high), NN)
    ladder = both[:height] + both[height:] + dot(amps_ref[:height], blocks(low), NN)
    for load in loads:
        load.wait()
    held[...] += ladder
    stores = [
        pltpu.make_async_copy(held.at[:, n * size : (n + 1) * size], out_ref.at[:, 0, place], sems.at[n])
        for n, place in enumerate(places)
    ]
    for store in stores:
        store.start()
    for store in stores:
        store.wait()


def ladder(meta, amps, masks, pieces, base, depth):
    height, size = base.shape[0], pieces[0].shape[1]
    vmem, hbm = pl.BlockSpec(memory_space=pltpu.VMEM), pl.BlockSpec(memory_space=pl.ANY)
    columns = size * len(pieces)
    return pl.pallas_call(
        functools.partial(ladder_kernel, depth, masks),
        out_shape=jax.ShapeDtypeStruct(base.shape, base.dtype),
        in_specs=[vmem, vmem] + [vmem] * len(pieces) + [hbm],
        out_specs=hbm,
        scratch_shapes=[pltpu.VMEM((height, columns), jnp.float32), pltpu.SemaphoreType.DMA((len(pieces),))],
        input_output_aliases={2 + len(pieces): 0},
        compiler_params=pltpu.CompilerParams(vmem_limit_bytes=48 << 20),
        cost_estimate=pl.CostEstimate(
            flops=6 * height * columns * GROUP * depth, bytes_accessed=8 * height * columns, transcendentals=0
        ),
        name="ladder",
    )(meta, amps, *pieces, base)


def swap(values, axis, size, mask):
    return lax.ppermute(values, axis, [(device, device ^ mask) for device in range(size)])


def spread_tiles(amps, size):
    tiles = {0: amps}
    bit = size >> 1
    while bit:
        for number in sorted(tiles):
            tiles[number | bit] = swap(tiles[number], "vir", size, bit)
        bit >>= 1
    return [tiles[number] for number in range(size)]


def shards(occ_size, vir_size, amps, resid, ints, tasks, pair_tiles, irreps):
    rows = ints[0]
    height, width = rows.shape
    depth = min(DEPTH, width)

    def exchange(buf):
        if height % LANES:
            return [((0,), [lax.all_gather(buf, "occ", axis=1, tiled=True)])]
        near = {0: buf}
        for mask in range(2, occ_size, 2):
            near[mask] = swap(buf, "occ", occ_size, mask)
        far = {mask | 1: swap(piece, "occ", occ_size, 1) for mask, piece in near.items()} if occ_size > 1 else {}
        return [(tuple(part), list(part.values())) for part in (near, far) if part]

    def add_round(first, base, tiles):
        buf, meta = prep(first, tasks, pair_tiles, irreps, rows, depth)
        groups = exchange(buf)
        ordered, most = order(tasks, pair_tiles, irreps, meta, tiles, depth)
        for masks, pieces in groups:
            base = ladder(meta, ordered, masks, pieces, base, depth)
        return base, most

    tiles = spread_tiles(amps, vir_size)
    out, most = add_round(jnp.zeros((1,), jnp.int32), resid, tiles)

    def more(state):
        return state[0][0] < most[0]

    def again(state):
        first, base = state
        return first + depth, add_round(first, base, tiles)[0]

    return lax.while_loop(more, again, (jnp.full((1,), depth, jnp.int32), out))[1]


def solution(mesh):
    in_specs = (P("occ", "vir", None), P("occ", "vir", None), P("vir", "occ", None), P(), P(), P())
    out_specs = P("occ", "vir", None)
    body = functools.partial(shards, mesh.shape["occ"], mesh.shape["vir"])
    return jax.shard_map(body, mesh=mesh, in_specs=in_specs, out_specs=out_specs, check_vma=False)
```

time: 101 us -> 40 us (0.40)
  waiting for transfers between devices: 60.1 us -> 18.7 us
  between operations: 15.4 us -> 0.09 us
  matrix products: 6.62 us -> 0 us
  Pallas kernels: 0 us -> 6.05 us
  other arithmetic: 5.77 us -> 0 us
  starting transfers between devices: 7.73 us -> 12.7 us
  local copies, waits for them, and re-layouts: 4.84 us -> 1.54 us
    all_gather x1 -> x0, waiting for transfers between devices: 50.8 us -> none  [shards(): lax.all_gather(ints, 'occ', axis=1, tiled=True)[0]]
    ppermute x0 -> x10, waiting for transfers between devices: none -> 18.7 us  [swap(): lax.ppermute(values, axis, [(device, device ^ mask) for device in range(s...]
    ppermute x0 -> x10, starting transfers between devices: none -> 12.7 us  [swap(): lax.ppermute(values, axis, [(device, device ^ mask) for device in range(s...]
    all_to_all x2 -> x0, waiting for transfers between devices: 8.56 us -> none  [the longest x1 8.56 us: shards(): lax.all_to_all(picked, 'vir', split_axis=1, concat_axis=0, tiled=True)]
    all_to_all x2 -> x0, starting transfers between devices: 7.73 us -> none  [the longest x1 4.25 us: shards(): lax.all_to_all(amps, 'vir', split_axis=0, concat_axis=1, tiled=True)]
    dot_general x1 -> x0, matrix products: 6.62 us -> none  [contract(): lax.dot_general(left, right, (((1,), (1,)), ((), ())), precision=lax.Prec...]
    pallas_call x0 -> x4, Pallas kernels: none -> 6.05 us  [the longest x2 2.47 us: ladder(): pl.pallas_call(functools.partial(ladder_kernel, depth, masks), out_shape=...]
    eq x4 -> x0, other arithmetic: 2.58 us -> none  [the longest x2 1.31 us: tile_irreps(): tile_ids[:, None] == tile_pair[1]]
  transfers between devices with their start and end apart: 3 -> 10, of which waited for: 2 -> 3; matrix products, arithmetic and copies ran while one was open for 9% -> 0% of each run, Pallas kernels for 0% -> 12%
where the time goes in v1:
time: 40 us; the launch traced here: 39.9 us
  waiting for transfers between devices  18.7 us (47%)
  starting transfers between devices  12.7 us (32%)
  Pallas kernels  6.05 us (15%)
  local copies, waits for them, and re-layouts  1.54 us (4%)
  loops' own time  0.87 us (2%)
    ppermute x10, waiting for transfers between devices, swap(): lax.ppermute(values, axis, [(device, device ^ mask) for device in range(s...  18.7 us
    ppermute x10, starting transfers between devices, swap(): lax.ppermute(values, axis, [(device, device ^ mask) for device in range(s...  12.7 us
    pallas_call x2, Pallas kernels, ladder(): pl.pallas_call(functools.partial(ladder_kernel, depth, masks), out_shape=...  2.47 us
    pallas_call x1, Pallas kernels, order(): pl.pallas_call(functools.partial(order_kernel, depth, len(tiles)), out_sh...  2.33 us
    unnamed x15, local copies, waits for them, and re-layouts  1.54 us
    pallas_call x1, Pallas kernels, prep(): pl.pallas_call(functools.partial(prep_kernel, depth), out_shape=(jax.Shap...  1.26 us
    another operation x1, loops' own time, shards(): lax.while_loop(more, again, (jnp.full((1,), depth, jnp.int32), out))[1]  0.87 us
  transfers between devices with their start and end apart: 10, of which 3 were waited for; matrix products, arithmetic and copies ran while one was open for 0% of the time, Pallas kernels for 12%

profile of v1, /device:TPU:0, one launch (start us, length us, event | category | flops | bytes accessed | tf_op | source)
XLA Modules:
  0.0 39.9 jit_solution(10082426333094904304)
XLA Ops:
  0.0 0.0 copy-start.5
  0.0 0.0 copy-start.2
  0.0 0.0 copy-start.3
  0.0 3.0 %collective-permute-start.8 = (f32[128,1,1024]{2,1,0:T(1,128)}, f32[128,1,1024]{2,1,0:T(1,128)S(1)}, u32[]{:S(2)}, u32[]{:S(2)}) collective-permute-start(f32[128,1,1024]{2,1,0:T(1,128)} %refs_4_.2), channel_id=1, source_target_pairs={{0,2},{1,3},{2,0},{3,1},{4,6},{5,7},{6,4},{7,5},{8,10},{9,11},{10,... | collective-permute-start | bytes 1572872 | tf_op jit(solution)/shard_map/ppermute | solution.py:204
  3.0 0.0 collective-permute-start.7
  3.0 12.1 %collective-permute-done.8.refs_6_ = f32[128,1,1024]{2,1,0:T(1,128)S(1)} collective-permute-done((f32[128,1,1024]{2,1,0:T(1,128)}, f32[128,1,1024]{2,1,0:T(1,128)S(1)}, u32[]{:S(2)}, u32[]{:S(2)}) %collective-permute-start.8) | collective-permute-done | bytes 524320 | tf_op jit(solution)/shard_map/ppermute | solution.py:204
  15.2 0.0 collective-permute-start.9
  15.2 0.0 copy-done.5
  15.2 0.1 copy.11.pairs_ref.refs_1_
  15.3 0.0 copy-start.4
  15.3 0.0 copy-start.6
  15.3 0.0 copy-done.2
  15.3 0.0 copy-done.3
  15.3 0.6 %copy-done.4 = s32[4]{0:T(128)S(1)} copy-done((s32[4]{0:T(128)S(1)}, s32[4]{0:T(128)}, u32[]{:S(2)}) %copy-start.4) | copy-done | bytes 40
  15.9 1.3 %compact.2 = (f32[192,128]{1,0:T(8,128)S(1)}, s32[8,1024]{1,0:T(8,128)S(1)}) custom-call(s32[1]{0:T(128)} %constant.2.clone.1.first_ref, s32[4]{0:T(128)S(1)} %copy-done.4, s32[4,2]{1,0:T(4,128)S(1)} %copy.11.pairs_ref.refs_1_, s32[19,32]{1,0:T(8,128)S(1)} %copy-done.3, f32[128,1024]{1,0:T(8,128)S(1)} %bitcast.3), custom_call_target="tpu_custom_call" | custom-call | flops 100663296 | bytes 524288 | tf_op jit(solution)/shard_map/compact/pallas_call | solution.py:87
  17.2 1.9 %collective-permute-start.11 = (f32[192,128]{1,0:T(8,128)S(1)}, f32[192,128]{1,0:T(8,128)S(1)}, u32[]{:S(2)}, u32[]{:S(2)}) collective-permute-start(f32[192,128]{1,0:T(8,128)S(1)} %get-tuple-element.72.refs_0_), channel_id=1, source_target_pairs={{0,8},{4,12},{8,0},{12,4},{16,24},{20,28},{24,16},{28,20},{1,9},{5... | collective-permute-start | bytes 294920 | tf_op jit(solution)/shard_map/ppermute | solution.py:204
  19.0 2.6 %collective-permute-start.13 = (f32[192,128]{1,0:T(8,128)S(1)}, f32[192,128]{1,0:T(8,128)S(1)}, u32[]{:S(2)}, u32[]{:S(2)}) collective-permute-start(f32[192,128]{1,0:T(8,128)S(1)} %get-tuple-element.72.refs_0_), channel_id=1, source_target_pairs={{0,16},{4,20},{8,24},{12,28},{16,0},{20,4},{24,8},{28,12},{1,17},{... | collective-permute-start | bytes 294920 | tf_op jit(solution)/shard_map/ppermute | solution.py:204
  21.6 0.0 collective-permute-start.15
  21.6 0.9 %collective-permute-done.11.refs_1_ = f32[192,128]{1,0:T(8,128)S(1)} collective-permute-done((f32[192,128]{1,0:T(8,128)S(1)}, f32[192,128]{1,0:T(8,128)S(1)}, u32[]{:S(2)}, u32[]{:S(2)}) %collective-permute-start.11) | collective-permute-done | bytes 98336 | tf_op jit(solution)/shard_map/ppermute | solution.py:204
  22.5 1.7 %collective-permute-start.10 = (f32[192,128]{1,0:T(8,128)S(1)}, f32[192,128]{1,0:T(8,128)S(1)}, u32[]{:S(2)}, u32[]{:S(2)}) collective-permute-start(f32[192,128]{1,0:T(8,128)S(1)} %get-tuple-element.72.refs_0_), channel_id=1, source_target_pairs={{0,4},{4,0},{8,12},{12,8},{16,20},{20,16},{24,28},{28,24},{1,5},{5... | collective-permute-start | bytes 294920 | tf_op jit(solution)/shard_map/ppermute | solution.py:204
  24.2 5.6 %collective-permute-done.13.refs_2_ = f32[192,128]{1,0:T(8,128)S(1)} collective-permute-done((f32[192,128]{1,0:T(8,128)S(1)}, f32[192,128]{1,0:T(8,128)S(1)}, u32[]{:S(2)}, u32[]{:S(2)}) %collective-permute-start.13) | collective-permute-done | bytes 98336 | tf_op jit(solution)/shard_map/ppermute | solution.py:204
  29.8 1.5 %collective-permute-start.12 = (f32[192,128]{1,0:T(8,128)S(1)}, f32[192,128]{1,0:T(8,128)S(1)}, u32[]{:S(2)}, u32[]{:S(2)}) collective-permute-start(f32[192,128]{1,0:T(8,128)S(1)} %collective-permute-done.11.refs_1_), channel_id=1, source_target_pairs={{0,4},{4,0},{8,12},{12,8},{16,20},{20,16},{24,28},{28,24},{1,5},{5... | collective-permute-start | bytes 294920 | tf_op jit(solution)/shard_map/ppermute | solution.py:204
  31.3 0.0 collective-permute-done.15.refs_3_
  31.3 0.5 %collective-permute-start.14 = (f32[192,128]{1,0:T(8,128)S(1)}, f32[192,128]{1,0:T(8,128)S(1)}, u32[]{:S(2)}, u32[]{:S(2)}) collective-permute-start(f32[192,128]{1,0:T(8,128)S(1)} %collective-permute-done.13.refs_2_), channel_id=1, source_target_pairs={{0,4},{4,0},{8,12},{12,8},{16,20},{20,16},{24,28},{28,24},{1,5},{5... | collective-permute-start | bytes 294920 | tf_op jit(solution)/shard_map/ppermute | solution.py:204
  31.8 0.0 collective-permute-done.7.refs_5_
  31.8 1.5 %collective-permute-start.16 = (f32[192,128]{1,0:T(8,128)S(1)}, f32[192,128]{1,0:T(8,128)S(1)}, u32[]{:S(2)}, u32[]{:S(2)}) collective-permute-start(f32[192,128]{1,0:T(8,128)S(1)} %collective-permute-done.15.refs_3_), channel_id=1, source_target_pairs={{0,4},{4,0},{8,12},{12,8},{16,20},{20,16},{24,28},{28,24},{1,5},{5... | collective-permute-start | bytes 294920 | tf_op jit(solution)/shard_map/ppermute | solution.py:204
  33.3 0.0 collective-permute-done.9.refs_7_
  33.3 0.0 copy-done.6
  33.3 0.0 copy-start.1
  33.3 2.3 %order_amplitudes.2 = (bf16[256,1536]{1,0:T(8,128)(2,1)S(1)}, s32[1]{0:T(128)}) custom-call(s32[4]{0:T(128)S(1)} %copy-done.4, s32[4,2]{1,0:T(4,128)S(1)} %copy.11.pairs_ref.refs_1_, s32[19,32]{1,0:T(8,128)S(1)} %copy-done.3, s32[8,1024]{1,0:T(8,128)S(1)} %get-tuple-element.70.refs_3_.meta_ref, f32[128,1,1024]{2,1,0:T(1,128)S(1)} %copy-done.6, ...), custom_call_target="tpu_custom_call" | custom-call | flops 805306368 | bytes 524288 | tf_op jit(solution)/shard_map/order_amplitudes/pallas_call | solution.py:135
  35.7 0.0 copy-done.1
  35.7 1.2 %ladder.4.refs_4_ = f32[128,1,1024]{2,1,0:T(1,128)S(1)} custom-call(s32[8,1024]{1,0:T(8,128)S(1)} %get-tuple-element.70.refs_3_.meta_ref, bf16[256,1536]{1,0:T(8,128)(2,1)S(1)} %get-tuple-element.71.amps_ref, f32[192,128]{1,0:T(8,128)S(1)} %get-tuple-element.72.refs_0_, ...), custom_call_target="tpu_custom_call", output_to_operand_aliasing={{}: (6, {})} | custom-call | flops 603979776 | bytes 524288 | tf_op jit(solution)/shard_map/ladder/pallas_call | solution.py:188
  36.9 0.0 collective-permute-done.10.refs_0_
  36.9 0.0 collective-permute-done.12.refs_1_
  36.9 0.0 collective-permute-done.14.refs_2_
  36.9 0.0 collective-permute-done.16.refs_3_
  37.0 1.2 %ladder.5 = f32[128,1,1024]{2,1,0:T(1,128)S(1)} custom-call(s32[8,1024]{1,0:T(8,128)S(1)} %get-tuple-element.70.refs_3_.meta_ref, bf16[256,1536]{1,0:T(8,128)(2,1)S(1)} %get-tuple-element.71.amps_ref, f32[192,128]{1,0:T(8,128)S(1)} %collective-permute-done.10.refs_0_, ...), custom_call_target="tpu_custom_call", output_to_operand_aliasing={{}: (6, {})} | custom-call | flops 603979776 | bytes 524288 | tf_op jit(solution)/shard_map/ladder/pallas_call | solution.py:188
  38.2 0.9 %while.10 = (s32[1]{0:T(128)}, f32[128,1,1024]{2,1,0:T(1,128)S(1)}, s32[1]{0:T(128)}, s32[4]{0:T(128)S(1)}, s32[4,2]{1,0:T(4,128)S(1)}, /*index=5*/s32[19,32]{1,...) while((s32[1]{0:T(128)}, f32[128,1,1024]{2,1,0:T(1,128)S(1)}, ...), condition=%wide.region_1.0_spmd, body=%wide.region_0.0_spmd | while | flops 2113929216 | bytes 4850061 | solution.py:249
  39.1 0.0 copy-start
  39.1 0.8 %copy-done = f32[128,1,1024]{2,1,0:T(1,128)} copy-done((f32[128,1,1024]{2,1,0:T(1,128)}, f32[128,1,1024]{2,1,0:T(1,128)S(1)}, u32[]{:S(2)}) %copy-start) | copy-done | bytes 524312
Async XLA Ops:
  0.0 15.2 %copy-start.5 = (s32[4,2]{0,1:T(2,128)S(1)}, s32[4,2]{0,1:T(2,128)}, u32[]{:S(2)}) copy-start(s32[4,2]{0,1:T(2,128)} %param.12) | copy-start | bytes 100
  0.0 15.3 %copy-start.2 = (f32[1,128,1024]{2,1,0:T(8,128)S(1)}, f32[1,128,1024]{2,1,0:T(8,128)}, u32[]{:S(2)}) copy-start(f32[1,128,1024]{2,1,0:T(8,128)} %param.10) | copy-start | bytes 1572868
  0.0 15.3 %copy-start.3 = (s32[19,32]{1,0:T(8,128)S(1)}, s32[19,32]{1,0:T(8,128)}, u32[]{:S(2)}) copy-start(s32[19,32]{1,0:T(8,128)} %refs_2_.1) | copy-start | bytes 7300
  0.0 15.2 %collective-permute-start.8 = (f32[128,1,1024]{2,1,0:T(1,128)}, f32[128,1,1024]{2,1,0:T(1,128)S(1)}, u32[]{:S(2)}, u32[]{:S(2)}) collective-permute-start(f32[128,1,1024]{2,1,0:T(1,128)} %refs_4_.2), channel_id=1, source_target_pairs={{0,2},{1,3},{2,0},{3,1},{4,6},{5,7},{6,4},{7,5},{8,10},{9,11},{10,... | collective-permute-start | bytes 1572872 | tf_op jit(solution)/shard_map/ppermute | solution.py:204
  3.0 28.8 %collective-permute-start.7 = (f32[128,1,1024]{2,1,0:T(1,128)}, f32[128,1,1024]{2,1,0:T(1,128)S(1)}, u32[]{:S(2)}, u32[]{:S(2)}) collective-permute-start(f32[128,1,1024]{2,1,0:T(1,128)} %refs_4_.2), channel_id=1, source_target_pairs={{0,1},{1,0},{2,3},{3,2},{4,5},{5,4},{6,7},{7,6},{8,9},{9,8},{10,11... | collective-permute-start | bytes 1572872 | tf_op jit(solution)/shard_map/ppermute | solution.py:204
  15.2 18.1 %collective-permute-start.9 = (f32[128,1,1024]{2,1,0:T(1,128)S(1)}, f32[128,1,1024]{2,1,0:T(1,128)S(1)}, u32[]{:S(2)}, u32[]{:S(2)}) collective-permute-start(f32[128,1,1024]{2,1,0:T(1,128)S(1)} %collective-permute-done.8.refs_6_), channel_id=1, source_target_pairs={{0,1},{1,0},{2,3},{3,2},{4,5},{5,4},{6,7},{7,6},{8,9},{9,8},{10,11... | collective-permute-start | bytes 1572872 | tf_op jit(solution)/shard_map/ppermute | solution.py:204
  15.3 0.7 %copy-start.4 = (s32[4]{0:T(128)S(1)}, s32[4]{0:T(128)}, u32[]{:S(2)}) copy-start(s32[4]{0:T(128)} %refs_0_.1) | copy-start | bytes 52
  15.3 18.0 %copy-start.6 = (f32[128,1,1024]{2,1,0:T(1,128)S(1)}, f32[128,1,1024]{2,1,0:T(1,128)}, u32[]{:S(2)}) copy-start(f32[128,1,1024]{2,1,0:T(1,128)} %refs_4_.2) | copy-start | bytes 1572868
  17.2 5.3 %collective-permute-start.11 = (f32[192,128]{1,0:T(8,128)S(1)}, f32[192,128]{1,0:T(8,128)S(1)}, u32[]{:S(2)}, u32[]{:S(2)}) collective-permute-start(f32[192,128]{1,0:T(8,128)S(1)} %get-tuple-element.72.refs_0_), channel_id=1, source_target_pairs={{0,8},{4,12},{8,0},{12,4},{16,24},{20,28},{24,16},{28,20},{1,9},{5... | collective-permute-start | bytes 294920 | tf_op jit(solution)/shard_map/ppermute | solution.py:204
  19.0 10.7 %collective-permute-start.13 = (f32[192,128]{1,0:T(8,128)S(1)}, f32[192,128]{1,0:T(8,128)S(1)}, u32[]{:S(2)}, u32[]{:S(2)}) collective-permute-start(f32[192,128]{1,0:T(8,128)S(1)} %get-tuple-element.72.refs_0_), channel_id=1, source_target_pairs={{0,16},{4,20},{8,24},{12,28},{16,0},{20,4},{24,8},{28,12},{1,17},{... | collective-permute-start | bytes 294920 | tf_op jit(solution)/shard_map/ppermute | solution.py:204
  21.6 9.6 %collective-permute-start.15 = (f32[192,128]{1,0:T(8,128)S(1)}, f32[192,128]{1,0:T(8,128)S(1)}, u32[]{:S(2)}, u32[]{:S(2)}) collective-permute-start(f32[192,128]{1,0:T(8,128)S(1)} %get-tuple-element.72.refs_0_), channel_id=1, source_target_pairs={{0,24},{4,28},{8,16},{12,20},{16,8},{20,12},{24,0},{28,4},{1,25},{... | collective-permute-start | bytes 294920 | tf_op jit(solution)/shard_map/ppermute | solution.py:204
  22.5 14.4 %collective-permute-start.10 = (f32[192,128]{1,0:T(8,128)S(1)}, f32[192,128]{1,0:T(8,128)S(1)}, u32[]{:S(2)}, u32[]{:S(2)}) collective-permute-start(f32[192,128]{1,0:T(8,128)S(1)} %get-tuple-element.72.refs_0_), channel_id=1, source_target_pairs={{0,4},{4,0},{8,12},{12,8},{16,20},{20,16},{24,28},{28,24},{1,5},{5... | collective-permute-start | bytes 294920 | tf_op jit(solution)/shard_map/ppermute | solution.py:204
  29.8 7.1 %collective-permute-start.12 = (f32[192,128]{1,0:T(8,128)S(1)}, f32[192,128]{1,0:T(8,128)S(1)}, u32[]{:S(2)}, u32[]{:S(2)}) collective-permute-start(f32[192,128]{1,0:T(8,128)S(1)} %collective-permute-done.11.refs_1_), channel_id=1, source_target_pairs={{0,4},{4,0},{8,12},{12,8},{16,20},{20,16},{24,28},{28,24},{1,5},{5... | collective-permute-start | bytes 294920 | tf_op jit(solution)/shard_map/ppermute | solution.py:204
  31.3 5.7 %collective-permute-start.14 = (f32[192,128]{1,0:T(8,128)S(1)}, f32[192,128]{1,0:T(8,128)S(1)}, u32[]{:S(2)}, u32[]{:S(2)}) collective-permute-start(f32[192,128]{1,0:T(8,128)S(1)} %collective-permute-done.13.refs_2_), channel_id=1, source_target_pairs={{0,4},{4,0},{8,12},{12,8},{16,20},{20,16},{24,28},{28,24},{1,5},{5... | collective-permute-start | bytes 294920 | tf_op jit(solution)/shard_map/ppermute | solution.py:204
  31.8 5.1 %collective-permute-start.16 = (f32[192,128]{1,0:T(8,128)S(1)}, f32[192,128]{1,0:T(8,128)S(1)}, u32[]{:S(2)}, u32[]{:S(2)}) collective-permute-start(f32[192,128]{1,0:T(8,128)S(1)} %collective-permute-done.15.refs_3_), channel_id=1, source_target_pairs={{0,4},{4,0},{8,12},{12,8},{16,20},{20,16},{24,28},{28,24},{1,5},{5... | collective-permute-start | bytes 294920 | tf_op jit(solution)/shard_map/ppermute | solution.py:204
  33.3 2.3 %copy-start.1 = (f32[128,1,1024]{2,1,0:T(1,128)S(1)}, f32[128,1,1024]{2,1,0:T(1,128)}, u32[]{:S(2)}) copy-start(f32[128,1,1024]{2,1,0:T(1,128)} %param.9) | copy-start | bytes 1572868
  39.1 0.8 %copy-start = (f32[128,1,1024]{2,1,0:T(1,128)}, f32[128,1,1024]{2,1,0:T(1,128)S(1)}, u32[]{:S(2)}) copy-start(f32[128,1,1024]{2,1,0:T(1,128)S(1)} %get-tuple-element.232) | copy-start | bytes 1572868

commit v2 on v1

--- a/solution.py
+++ b/solution.py
@@ -98,20 +98,7 @@
     )(first, tasks, pairs, irreps, ints)
 
 
-def order_kernel(depth, count, *refs):
-    tasks_ref, pairs_ref, irreps_ref, meta_ref = refs[:4]
-    tiles, (out_ref, most_ref, held, sem) = refs[4 : 4 + count], refs[4 + count :]
-    own = lax.axis_index("vir")
-    chosen = jnp.bitwise_xor(tasks_ref[own], own)
-    for number, tile_ref in enumerate(tiles):
-
-        @pl.when(chosen == number)
-        def _(tile_ref=tile_ref):
-            copy = pltpu.make_async_copy(tile_ref.at[:, 0, :], held, sem)
-            copy.start()
-            copy.wait()
-
-    width = meta_ref.shape[1]
+def count_kernel(width, tasks_ref, pairs_ref, irreps_ref, most_ref):
     rows = lambda side: jnp.concatenate(
         [irreps_ref[pl.ds(pairs_ref[tasks_ref[k], side], 1), :] for k in range(tasks_ref.shape[0])], axis=0
     )
@@ -121,40 +108,58 @@
         most = jnp.maximum(most, jnp.sum((irrep == g).astype(jnp.int32), axis=1, keepdims=True))
     most_ref[0] = jnp.max(most)
 
-    high, low = split(held[...])
-    both = jnp.concatenate([high, low], axis=0)
-    for at in range(0, GROUP * depth, GROUP * depth // 4):
-        size = GROUP * depth // 4
-        place = (iota((size, width), 0) + at == meta_ref[:1]).astype(jnp.bfloat16)
+
+def count(tasks, pairs, irreps, width):
+    smem, vmem = pl.BlockSpec(memory_space=pltpu.SMEM), pl.BlockSpec(memory_space=pltpu.VMEM)
+    return pl.pallas_call(
+        functools.partial(count_kernel, width),
+        out_shape=jax.ShapeDtypeStruct((1,), jnp.int32),
+        in_specs=[smem, smem, vmem],
+        out_specs=smem,
+        name="count",
+    )(tasks, pairs, irreps)
+
+
+def order_kernel(depth, count, *refs):
+    tasks_ref, meta_ref = refs[:2]
+    tiles, (out_ref, held, sem) = refs[2 : 2 + count], refs[2 + count :]
+    own = lax.axis_index("vir")
+    chosen = jnp.bitwise_xor(tasks_ref[own], own)
+    copies = [pltpu.make_async_copy(tile_ref.at[:, 0, :], held, sem) for tile_ref in tiles]
+    for number, copy in enumerate(copies):
+        pl.when(chosen == number)(copy.start)
+    width, size = meta_ref.shape[1], GROUP * depth // 4
+    starts = range(0, GROUP * depth, size)
+    places = [(iota((size, width), 0) + at == meta_ref[:1]).astype(jnp.bfloat16) for at in starts]
+    copies[0].wait()
+    both = jnp.concatenate(split(held[...]), axis=0)
+    for at, place in zip(starts, places):
         out_ref[:, at : at + size] = dot(both, place, NT).astype(jnp.bfloat16)
 
 
-def order(tasks, pairs, irreps, meta, tiles, depth):
+def order(tasks, meta, tiles, depth):
     height, _, width = tiles[0].shape
     smem, vmem = pl.BlockSpec(memory_space=pltpu.SMEM), pl.BlockSpec(memory_space=pltpu.VMEM)
     return pl.pallas_call(
         functools.partial(order_kernel, depth, len(tiles)),
-        out_shape=(
-            jax.ShapeDtypeStruct((2 * height, GROUP * depth), jnp.bfloat16),
-            jax.ShapeDtypeStruct((1,), jnp.int32),
-        ),
-        in_specs=[smem, smem, vmem, vmem] + [pl.BlockSpec(memory_space=pl.ANY)] * len(tiles),
-        out_specs=(vmem, smem),
+        out_shape=jax.ShapeDtypeStruct((2 * height, GROUP * depth), jnp.bfloat16),
+        in_specs=[smem, vmem] + [pl.BlockSpec(memory_space=pl.ANY)] * len(tiles),
+        out_specs=vmem,
         scratch_shapes=[pltpu.VMEM((height, width), jnp.float32), pltpu.SemaphoreType.DMA],
         compiler_params=pltpu.CompilerParams(vmem_limit_bytes=32 << 20),
         cost_estimate=pl.CostEstimate(
             flops=4 * height * width * GROUP * depth, bytes_accessed=4 * height * width, transcendentals=0
         ),
         name="order_amplitudes",
-    )(tasks, pairs, irreps, meta, *tiles)
-
-
-def ladder_kernel(depth, masks, meta_ref, amps_ref, *refs):
-    count = len(masks)
-    pieces, (base_ref, out_ref, held, sems) = refs[:count], refs[count:]
+    )(tasks, meta, *tiles)
+
+
+def ladder_kernel(depth, masks, count, meta_ref, amps_ref, *refs):
+    pieces, base_ref, (out_ref, held, sems) = refs[:count], refs[count], refs[-3:]
     block = lax.axis_index("occ")
     height = held.shape[0]
     size = pieces[0].shape[1]
+    pieces = [piece.at[at : at + depth] for piece in pieces for at in range(0, piece.shape[0], depth)]
     places = [pl.ds(pl.multiple_of(jnp.bitwise_xor(block, mask) * size, LANES), size) for mask in masks]
     loads = [
         pltpu.make_async_copy(base_ref.at[:, 0, place], held.at[:, n * size : (n + 1) * size], sems.at[n])
@@ -181,32 +186,36 @@
         store.wait()
 
 
-def ladder(meta, amps, masks, pieces, base, depth):
+def ladder(meta, amps, masks, pieces, base, out, depth):
+    into = () if out is None else (out,)
     height, size = base.shape[0], pieces[0].shape[1]
     vmem, hbm = pl.BlockSpec(memory_space=pltpu.VMEM), pl.BlockSpec(memory_space=pl.ANY)
-    columns = size * len(pieces)
-    return pl.pallas_call(
-        functools.partial(ladder_kernel, depth, masks),
+    columns = size * len(masks)
+    return pl.pallas_call(
+        functools.partial(ladder_kernel, depth, masks, len(pieces)),
         out_shape=jax.ShapeDtypeStruct(base.shape, base.dtype),
-        in_specs=[vmem, vmem] + [vmem] * len(pieces) + [hbm],
+        in_specs=[vmem, vmem] + [vmem] * len(pieces) + [hbm] * (1 + len(into)),
         out_specs=hbm,
-        scratch_shapes=[pltpu.VMEM((height, columns), jnp.float32), pltpu.SemaphoreType.DMA((len(pieces),))],
-        input_output_aliases={2 + len(pieces): 0},
+        scratch_shapes=[pltpu.VMEM((height, columns), jnp.float32), pltpu.SemaphoreType.DMA((len(masks),))],
+        input_output_aliases={3 + len(pieces): 0} if into else {},
         compiler_params=pltpu.CompilerParams(vmem_limit_bytes=48 << 20),
         cost_estimate=pl.CostEstimate(
             flops=6 * height * columns * GROUP * depth, bytes_accessed=8 * height * columns, transcendentals=0
         ),
         name="ladder",
-    )(meta, amps, *pieces, base)
+    )(meta, amps, *pieces, base, *into)
 
 
 def swap(values, axis, size, mask):
     return lax.ppermute(values, axis, [(device, device ^ mask) for device in range(size)])
 
 
-def spread_tiles(amps, size):
-    tiles = {0: amps}
-    bit = size >> 1
+def first_swaps(amps, size):
+    return {0: amps, size >> 1: swap(amps, "vir", size, size >> 1)}
+
+
+def other_swaps(tiles, size):
+    bit = size >> 2
     while bit:
         for number in sorted(tiles):
             tiles[number | bit] = swap(tiles[number], "vir", size, bit)
@@ -214,39 +223,51 @@
     return [tiles[number] for number in range(size)]
 
 
+def after(value, earlier):
+    return lax.optimization_barrier((value, earlier))[0]
+
+
+def exchange(buf, size):
+    lead = size >> 1
+    even = [lead] + [mask for mask in range(2, size, 2) if mask != lead] if size > 2 else []
+    near = {0: buf}
+    for mask in even:
+        near[mask] = swap(buf, "occ", size, mask) if mask <= lead else swap(near[mask & (mask - 1)], "occ", size, mask & -mask)
+    blocks = {(mask,): piece for mask, piece in near.items()}
+    groups = [(0,), tuple(even[-2::-1]), tuple(even[-1:])] if size > 1 else []
+    for group in groups:
+        if group:
+            whole = jnp.concatenate([near[mask] for mask in group], axis=0) if len(group) > 1 else near[group[0]]
+            blocks[tuple(mask | 1 for mask in group)] = swap(whole, "occ", size, 1)
+    return blocks, [piece for masks, piece in blocks.items() if len(masks) == 1 and masks[0] <= lead]
+
+
 def shards(occ_size, vir_size, amps, resid, ints, tasks, pair_tiles, irreps):
     rows = ints[0]
     height, width = rows.shape
     depth = min(DEPTH, width)
 
-    def exchange(buf):
-        if height % LANES:
-            return [((0,), [lax.all_gather(buf, "occ", axis=1, tiled=True)])]
-        near = {0: buf}
-        for mask in range(2, occ_size, 2):
-            near[mask] = swap(buf, "occ", occ_size, mask)
-        far = {mask | 1: swap(piece, "occ", occ_size, 1) for mask, piece in near.items()} if occ_size > 1 else {}
-        return [(tuple(part), list(part.values())) for part in (near, far) if part]
-
-    def add_round(first, base, tiles):
+    def add_round(first, base):
+        tiles = first_swaps(amps, vir_size)
         buf, meta = prep(first, tasks, pair_tiles, irreps, rows, depth)
-        groups = exchange(buf)
-        ordered, most = order(tasks, pair_tiles, irreps, meta, tiles, depth)
-        for masks, pieces in groups:
-            base = ladder(meta, ordered, masks, pieces, base, depth)
-        return base, most
-
-    tiles = spread_tiles(amps, vir_size)
-    out, most = add_round(jnp.zeros((1,), jnp.int32), resid, tiles)
-
-    def more(state):
-        return state[0][0] < most[0]
-
-    def again(state):
-        first, base = state
-        return first + depth, add_round(first, base, tiles)[0]
-
-    return lax.while_loop(more, again, (jnp.full((1,), depth, jnp.int32), out))[1]
+        if height % LANES or occ_size & (occ_size - 1):
+            blocks = {(0,): lax.all_gather(buf, "occ", axis=1, tiled=True)}
+            tiles = other_swaps(tiles, vir_size)
+        else:
+            blocks, direct = exchange(buf, occ_size)
+            tiles = {number: after(tile, direct) if number else tile for number, tile in tiles.items()}
+            tiles = other_swaps(tiles, vir_size)
+        tiles, base = lax.optimization_barrier((tiles, base))
+        ordered = order(tasks, meta, tiles, depth)
+        return ladder(meta, ordered, sum(blocks, ()), list(blocks.values()), base, None, depth)
+
+    most = count(tasks, pair_tiles, irreps, width)
+    rest = lax.while_loop(
+        lambda state: state[0][0] < most[0],
+        lambda state: (state[0] + depth, add_round(*state)),
+        (jnp.full((1,), depth, jnp.int32), resid),
+    )[1]
+    return add_round(jnp.zeros((1,), jnp.int32), rest)
 
 
 def solution(mesh):

time: 40 us -> 25.6 us (0.64)
  waiting for transfers between devices: 18.7 us -> 4.32 us
  Pallas kernels: 6.05 us -> 7.74 us
  local copies, waits for them, and re-layouts: 1.54 us -> 0.11 us
    ppermute x10 -> x9, waiting for transfers between devices: 18.7 us -> 4.32 us  [swap(): lax.ppermute(values, axis, [(device, device ^ mask) for device in range(s...]
    pallas_call x2, Pallas kernels: 2.47 us -> 4.05 us  [the longest x1 2.66 us: ladder(): pl.pallas_call(functools.partial(ladder_kernel, depth, masks, len(pieces)...]
    unnamed x15 -> x13, local copies, waits for them, and re-layouts: 1.54 us -> 0.11 us
    ppermute x10 -> x9, starting transfers between devices: 12.7 us -> 12.5 us  [swap(): lax.ppermute(values, axis, [(device, device ^ mask) for device in range(s...]
  transfers between devices with their start and end apart: 10 -> 9, of which waited for: 3 -> 4; matrix products, arithmetic and copies ran while one was open for 0% -> 0% of each run, Pallas kernels for 12% -> 20%
where the time goes in v2:
time: 25.6 us; the launch traced here: 25.5 us
  starting transfers between devices  12.5 us (49%)
  Pallas kernels  7.74 us (30%)
  waiting for transfers between devices  4.32 us (17%)
  loops' own time  0.68 us (3%)
    ppermute x9, starting transfers between devices, swap(): lax.ppermute(values, axis, [(device, device ^ mask) for device in range(s...  12.5 us
    ppermute x9, waiting for transfers between devices, swap(): lax.ppermute(values, axis, [(device, device ^ mask) for device in range(s...  4.32 us
    pallas_call x1, Pallas kernels, ladder(): pl.pallas_call(functools.partial(ladder_kernel, depth, masks, len(pieces)...  2.66 us
    pallas_call x1, Pallas kernels, order(): pl.pallas_call(functools.partial(order_kernel, depth, len(tiles)), out_sh...  2.43 us
    pallas_call x1, Pallas kernels, count(): pl.pallas_call(functools.partial(count_kernel, width), out_shape=jax.Shap...  1.39 us
    pallas_call x1, Pallas kernels, prep(): pl.pallas_call(functools.partial(prep_kernel, depth), out_shape=(jax.Shap...  1.26 us
    another operation x1, loops' own time, shards(): lax.while_loop(lambda state: state[0][0] < most[0], lambda state: (state[...  0.68 us
  transfers between devices with their start and end apart: 9, of which 4 were waited for; matrix products, arithmetic and copies ran while one was open for 0% of the time, Pallas kernels for 20%

profile of v2, /device:TPU:0, one launch (start us, length us, event | category | flops | bytes accessed | tf_op | source)
XLA Modules:
  0.0 25.5 jit_solution(11996568233454264919)
XLA Ops:
  0.0 0.0 copy-start.4
  0.0 0.0 copy-start
  0.0 0.0 copy-start.2
  0.0 0.0 copy-start.3
  0.0 0.0 copy-start.5
  0.0 0.0 copy-start.1
  0.0 3.0 %collective-permute-start.8 = (f32[128,1,1024]{2,1,0:T(1,128)}, f32[128,1,1024]{2,1,0:T(1,128)}, u32[]{:S(2)}, u32[]{:S(2)}) collective-permute-start(f32[128,1,1024]{2,1,0:T(1,128)} %refs_2_), channel_id=1, source_target_pairs={{0,2},{1,3},{2,0},{3,1},{4,6},{5,7},{6,4},{7,5},{8,10},{9,11},{10,... | collective-permute-start | bytes 1572872 | tf_op jit(solution)/shard_map/ppermute | solution.py:210
  3.1 0.0 collective-permute-start.7
  3.1 0.0 copy-done.4
  3.1 0.1 copy.7.pairs_ref
  3.2 0.0 copy-done
  3.2 0.0 copy-done.2
  3.2 0.0 copy-done.3
  3.2 1.3 %compact.3 = (f32[192,128]{1,0:T(8,128)S(1)}, s32[8,1024]{1,0:T(8,128)S(1)}) custom-call(s32[1]{0:T(128)} %constant.6.clone.1.first_ref, s32[4]{0:T(128)S(1)} %copy-done.3, s32[4,2]{1,0:T(4,128)S(1)} %copy.7.pairs_ref, s32[19,32]{1,0:T(8,128)S(1)} %copy-done.2, f32[128,1024]{1,0:T(8,128)S(1)} %bitcast.3), custom_call_target="tpu_custom_call" | custom-call | flops 100663296 | bytes 524288 | tf_op jit(solution)/shard_map/compact/pallas_call | solution.py:87
  4.4 2.6 %collective-permute-start.9 = (f32[192,128]{1,0:T(8,128)S(1)}, f32[192,128]{1,0:T(8,128)S(1)}, u32[]{:S(2)}, u32[]{:S(2)}) collective-permute-start(f32[192,128]{1,0:T(8,128)S(1)} %get-tuple-element.101.refs_0_), channel_id=1, source_target_pairs={{0,16},{4,20},{8,24},{12,28},{16,0},{20,4},{24,8},{28,12},{1,17},{... | collective-permute-start | bytes 294920 | tf_op jit(solution)/shard_map/ppermute | solution.py:210
  7.1 1.6 %collective-permute-start.10 = (f32[192,128]{1,0:T(8,128)S(1)}, f32[192,128]{1,0:T(8,128)S(1)}, u32[]{:S(2)}, u32[]{:S(2)}) collective-permute-start(f32[192,128]{1,0:T(8,128)S(1)} %get-tuple-element.101.refs_0_), channel_id=1, source_target_pairs={{0,8},{4,12},{8,0},{12,4},{16,24},{20,28},{24,16},{28,20},{1,9},{5... | collective-permute-start | bytes 294920 | tf_op jit(solution)/shard_map/ppermute | solution.py:210
  8.7 1.4 %count.1 = s32[1]{0:T(128)} custom-call(s32[4]{0:T(128)S(1)} %copy-done.3, s32[4,2]{1,0:T(4,128)S(1)} %copy.7.pairs_ref, s32[19,32]{1,0:T(8,128)S(1)} %copy-done.2), custom_call_target="tpu_custom_call" | custom-call | tf_op jit(solution)/shard_map/count/pallas_call | solution.py:114
  10.1 1.6 %collective-permute-start.11 = (f32[192,128]{1,0:T(8,128)S(1)}, f32[192,128]{1,0:T(8,128)S(1)}, u32[]{:S(2)}, u32[]{:S(2)}) collective-permute-start(f32[192,128]{1,0:T(8,128)S(1)} %get-tuple-element.101.refs_0_), channel_id=1, source_target_pairs={{0,4},{4,0},{8,12},{12,8},{16,20},{20,16},{24,28},{28,24},{1,5},{5... | collective-permute-start | bytes 294920 | tf_op jit(solution)/shard_map/ppermute | solution.py:210
  11.6 1.2 %collective-permute-done.9.refs_1_ = f32[192,128]{1,0:T(8,128)S(1)} collective-permute-done((f32[192,128]{1,0:T(8,128)S(1)}, f32[192,128]{1,0:T(8,128)S(1)}, u32[]{:S(2)}, u32[]{:S(2)}) %collective-permute-start.9) | collective-permute-done | bytes 98336 | tf_op jit(solution)/shard_map/ppermute | solution.py:210
  12.8 0.6 %collective-permute-start.13 = (f32[192,128]{1,0:T(8,128)S(1)}, f32[192,128]{1,0:T(8,128)S(1)}, u32[]{:S(2)}, u32[]{:S(2)}) collective-permute-start(f32[192,128]{1,0:T(8,128)S(1)} %collective-permute-done.9.refs_1_), channel_id=1, source_target_pairs={{0,8},{4,12},{8,0},{12,4},{16,24},{20,28},{24,16},{28,20},{1,9},{5... | collective-permute-start | bytes 294920 | tf_op jit(solution)/shard_map/ppermute | solution.py:210
  13.4 0.0 collective-permute-done.10.refs_2_
  13.4 1.6 %collective-permute-start.14 = (f32[384,128]{1,0:T(8,128)S(1)}, f32[384,128]{1,0:T(8,128)S(1)}, u32[]{:S(2)}, u32[]{:S(2)}) collective-permute-start(f32[384,128]{1,0:T(8,128)S(1)} %pad_maximum_fusion.1), channel_id=1, source_target_pairs={{0,4},{4,0},{8,12},{12,8},{16,20},{20,16},{24,28},{28,24},{1,5},{5... | collective-permute-start | bytes 589832 | tf_op jit(solution)/shard_map/ppermute | solution.py:210
  15.0 0.0 collective-permute-done.11.refs_4_
  15.0 0.3 %collective-permute-done.8.refs_4_ = f32[128,1,1024]{2,1,0:T(1,128)} collective-permute-done((f32[128,1,1024]{2,1,0:T(1,128)}, f32[128,1,1024]{2,1,0:T(1,128)}, u32[]{:S(2)}, u32[]{:S(2)}) %collective-permute-start.8) | collective-permute-done | bytes 524320 | tf_op jit(solution)/shard_map/ppermute | solution.py:210
  15.3 0.0 collective-permute-start.12
  15.3 2.1 %collective-permute-done.13.refs_3_ = f32[192,128]{1,0:T(8,128)S(1)} collective-permute-done((f32[192,128]{1,0:T(8,128)S(1)}, f32[192,128]{1,0:T(8,128)S(1)}, u32[]{:S(2)}, u32[]{:S(2)}) %collective-permute-start.13) | collective-permute-done | bytes 98336 | tf_op jit(solution)/shard_map/ppermute | solution.py:210
  17.4 0.0 collective-permute-done.7.refs_3_
  17.4 0.0 copy-done.5
  17.4 0.0 copy-done.1
  17.4 0.7 %while.11 = (s32[1]{0:T(128)}, f32[128,1,1024]{2,1,0:T(1,128)S(1)}, s32[1]{0:T(128)}, s32[4]{0:T(128)S(1)}, s32[4,2]{1,0:T(4,128)S(1)}, /*index=5*/s32[19,32]{1,...) while((s32[1]{0:T(128)}, f32[128,1,1024]{2,1,0:T(1,128)S(1)}, ...), condition=%wide.region_1.0_spmd, body=%wide.region_0.0_spmd | while | flops 2113978368 | bytes 8388997 | solution.py:265
  18.1 1.6 %collective-permute-start.15 = (f32[192,128]{1,0:T(8,128)S(1)}, f32[192,128]{1,0:T(8,128)S(1)}, u32[]{:S(2)}, u32[]{:S(2)}) collective-permute-start(f32[192,128]{1,0:T(8,128)S(1)} %collective-permute-done.13.refs_3_), channel_id=1, source_target_pairs={{0,4},{4,0},{8,12},{12,8},{16,20},{20,16},{24,28},{28,24},{1,5},{5... | collective-permute-start | bytes 294920 | tf_op jit(solution)/shard_map/ppermute | solution.py:210
  19.7 0.0 collective-permute-done.12.refs_5_
  19.7 2.4 %order_amplitudes.2.amps_ref = bf16[256,1536]{1,0:T(8,128)(2,1)S(1)} custom-call(s32[4]{0:T(128)S(1)} %get-tuple-element.258, s32[8,1024]{1,0:T(8,128)S(1)} %get-tuple-element.100.refs_1_.meta_ref, f32[128,1,1024]{2,1,0:T(1,128)S(1)} %get-tuple-element.261, f32[128,1,1024]{2,1,0:T(1,128)S(1)} %get-tuple-element.263, ...), custom_call_target="tpu_custom_call" | custom-call | flops 805306368 | bytes 524288 | tf_op jit(solution)/shard_map/order_amplitudes/pallas_call | solution.py:143
  22.1 0.0 collective-permute-done.14.refs_5_
  22.1 0.7 %collective-permute-done.15.refs_6_ = f32[192,128]{1,0:T(8,128)S(1)} collective-permute-done((f32[192,128]{1,0:T(8,128)S(1)}, f32[192,128]{1,0:T(8,128)S(1)}, u32[]{:S(2)}, u32[]{:S(2)}) %collective-permute-start.15) | collective-permute-done | bytes 98336 | tf_op jit(solution)/shard_map/ppermute | solution.py:210
  22.8 2.7 %ladder.3 = f32[128,1,1024]{2,1,0:T(1,128)} custom-call(s32[8,1024]{1,0:T(8,128)S(1)} %get-tuple-element.100.refs_1_.meta_ref, bf16[256,1536]{1,0:T(8,128)(2,1)S(1)} %order_amplitudes.2.amps_ref, f32[192,128]{1,0:T(8,128)S(1)} %get-tuple-element.101.refs_0_, f32[192,128]{1,0:T(8,128)S(1)} %collective-permute-done.9.refs_1_, ...), custom_call_target="tpu_custom_call" | custom-call | flops 1207959552 | bytes 1048576 | tf_op jit(solution)/shard_map/ladder/pallas_call | solution.py:194
  (1 shorter events, 0.0 us)
Async XLA Ops:
  0.0 3.1 %copy-start.4 = (s32[4,2]{0,1:T(2,128)S(1)}, s32[4,2]{0,1:T(2,128)}, u32[]{:S(2)}) copy-start(s32[4,2]{0,1:T(2,128)} %param.12) | copy-start | bytes 100
  0.0 3.2 %copy-start = (f32[1,128,1024]{2,1,0:T(8,128)S(1)}, f32[1,128,1024]{2,1,0:T(8,128)}, u32[]{:S(2)}) copy-start(f32[1,128,1024]{2,1,0:T(8,128)} %param.10) | copy-start | bytes 1572868
  0.0 3.2 %copy-start.2 = (s32[19,32]{1,0:T(8,128)S(1)}, s32[19,32]{1,0:T(8,128)}, u32[]{:S(2)}) copy-start(s32[19,32]{1,0:T(8,128)} %irreps_ref.3) | copy-start | bytes 7300
  0.0 3.2 %copy-start.3 = (s32[4]{0:T(128)S(1)}, s32[4]{0:T(128)}, u32[]{:S(2)}) copy-start(s32[4]{0:T(128)} %refs_0_.1) | copy-start | bytes 52
  0.0 17.4 %copy-start.5 = (f32[128,1,1024]{2,1,0:T(1,128)S(1)}, f32[128,1,1024]{2,1,0:T(1,128)}, u32[]{:S(2)}) copy-start(f32[128,1,1024]{2,1,0:T(1,128)} %refs_2_) | copy-start | bytes 1572868
  0.0 17.4 %copy-start.1 = (f32[128,1,1024]{2,1,0:T(1,128)S(1)}, f32[128,1,1024]{2,1,0:T(1,128)}, u32[]{:S(2)}) copy-start(f32[128,1,1024]{2,1,0:T(1,128)} %param.9) | copy-start | bytes 1572868
  0.0 15.3 %collective-permute-start.8 = (f32[128,1,1024]{2,1,0:T(1,128)}, f32[128,1,1024]{2,1,0:T(1,128)}, u32[]{:S(2)}, u32[]{:S(2)}) collective-permute-start(f32[128,1,1024]{2,1,0:T(1,128)} %refs_2_), channel_id=1, source_target_pairs={{0,2},{1,3},{2,0},{3,1},{4,6},{5,7},{6,4},{7,5},{8,10},{9,11},{10,... | collective-permute-start | bytes 1572872 | tf_op jit(solution)/shard_map/ppermute | solution.py:210
  3.1 14.4 %collective-permute-start.7 = (f32[128,1,1024]{2,1,0:T(1,128)}, f32[128,1,1024]{2,1,0:T(1,128)S(1)}, u32[]{:S(2)}, u32[]{:S(2)}) collective-permute-start(f32[128,1,1024]{2,1,0:T(1,128)} %refs_2_), channel_id=1, source_target_pairs={{0,1},{1,0},{2,3},{3,2},{4,5},{5,4},{6,7},{7,6},{8,9},{9,8},{10,11... | collective-permute-start | bytes 1572872 | tf_op jit(solution)/shard_map/ppermute | solution.py:210
  4.4 8.4 %collective-permute-start.9 = (f32[192,128]{1,0:T(8,128)S(1)}, f32[192,128]{1,0:T(8,128)S(1)}, u32[]{:S(2)}, u32[]{:S(2)}) collective-permute-start(f32[192,128]{1,0:T(8,128)S(1)} %get-tuple-element.101.refs_0_), channel_id=1, source_target_pairs={{0,16},{4,20},{8,24},{12,28},{16,0},{20,4},{24,8},{28,12},{1,17},{... | collective-permute-start | bytes 294920 | tf_op jit(solution)/shard_map/ppermute | solution.py:210
  7.1 6.3 %collective-permute-start.10 = (f32[192,128]{1,0:T(8,128)S(1)}, f32[192,128]{1,0:T(8,128)S(1)}, u32[]{:S(2)}, u32[]{:S(2)}) collective-permute-start(f32[192,128]{1,0:T(8,128)S(1)} %get-tuple-element.101.refs_0_), channel_id=1, source_target_pairs={{0,8},{4,12},{8,0},{12,4},{16,24},{20,28},{24,16},{28,20},{1,9},{5... | collective-permute-start | bytes 294920 | tf_op jit(solution)/shard_map/ppermute | solution.py:210
  10.1 4.9 %collective-permute-start.11 = (f32[192,128]{1,0:T(8,128)S(1)}, f32[192,128]{1,0:T(8,128)S(1)}, u32[]{:S(2)}, u32[]{:S(2)}) collective-permute-start(f32[192,128]{1,0:T(8,128)S(1)} %get-tuple-element.101.refs_0_), channel_id=1, source_target_pairs={{0,4},{4,0},{8,12},{12,8},{16,20},{20,16},{24,28},{28,24},{1,5},{5... | collective-permute-start | bytes 294920 | tf_op jit(solution)/shard_map/ppermute | solution.py:210
  12.8 4.6 %collective-permute-start.13 = (f32[192,128]{1,0:T(8,128)S(1)}, f32[192,128]{1,0:T(8,128)S(1)}, u32[]{:S(2)}, u32[]{:S(2)}) collective-permute-start(f32[192,128]{1,0:T(8,128)S(1)} %collective-permute-done.9.refs_1_), channel_id=1, source_target_pairs={{0,8},{4,12},{8,0},{12,4},{16,24},{20,28},{24,16},{28,20},{1,9},{5... | collective-permute-start | bytes 294920 | tf_op jit(solution)/shard_map/ppermute | solution.py:210
  13.4 8.7 %collective-permute-start.14 = (f32[384,128]{1,0:T(8,128)S(1)}, f32[384,128]{1,0:T(8,128)S(1)}, u32[]{:S(2)}, u32[]{:S(2)}) collective-permute-start(f32[384,128]{1,0:T(8,128)S(1)} %pad_maximum_fusion.1), channel_id=1, source_target_pairs={{0,4},{4,0},{8,12},{12,8},{16,20},{20,16},{24,28},{28,24},{1,5},{5... | collective-permute-start | bytes 589832 | tf_op jit(solution)/shard_map/ppermute | solution.py:210
  15.3 4.4 %collective-permute-start.12 = (f32[128,1,1024]{2,1,0:T(1,128)}, f32[128,1,1024]{2,1,0:T(1,128)S(1)}, u32[]{:S(2)}, u32[]{:S(2)}) collective-permute-start(f32[128,1,1024]{2,1,0:T(1,128)} %collective-permute-done.8.refs_4_), channel_id=1, source_target_pairs={{0,1},{1,0},{2,3},{3,2},{4,5},{5,4},{6,7},{7,6},{8,9},{9,8},{10,11... | collective-permute-start | bytes 1572872 | tf_op jit(solution)/shard_map/ppermute | solution.py:210
  18.1 4.7 %collective-permute-start.15 = (f32[192,128]{1,0:T(8,128)S(1)}, f32[192,128]{1,0:T(8,128)S(1)}, u32[]{:S(2)}, u32[]{:S(2)}) collective-permute-start(f32[192,128]{1,0:T(8,128)S(1)} %collective-permute-done.13.refs_3_), channel_id=1, source_target_pairs={{0,4},{4,0},{8,12},{12,8},{16,20},{20,16},{24,28},{28,24},{1,5},{5... | collective-permute-start | bytes 294920 | tf_op jit(solution)/shard_map/ppermute | solution.py:210

commit v3 on v2

--- a/solution.py
+++ b/solution.py
@@ -9,7 +9,7 @@
 
 GROUP = 8
 LANES = 128
-DEPTH = 192
+DEPTH = 176
 
 NT = (((1,), (1,)), ((), ()))
 NN = (((1,), (0,)), ((), ()))
@@ -128,13 +128,13 @@
     copies = [pltpu.make_async_copy(tile_ref.at[:, 0, :], held, sem) for tile_ref in tiles]
     for number, copy in enumerate(copies):
         pl.when(chosen == number)(copy.start)
-    width, size = meta_ref.shape[1], GROUP * depth // 4
-    starts = range(0, GROUP * depth, size)
-    places = [(iota((size, width), 0) + at == meta_ref[:1]).astype(jnp.bfloat16) for at in starts]
+    width, slots, size = meta_ref.shape[1], GROUP * depth, 3 * LANES
+    starts = range(0, slots, size)
+    places = [(iota((min(size, slots - at), width), 0) + at == meta_ref[:1]).astype(jnp.bfloat16) for at in starts]
     copies[0].wait()
     both = jnp.concatenate(split(held[...]), axis=0)
     for at, place in zip(starts, places):
-        out_ref[:, at : at + size] = dot(both, place, NT).astype(jnp.bfloat16)
+        out_ref[:, at : at + place.shape[0]] = dot(both, place, NT).astype(jnp.bfloat16)
 
 
 def order(tasks, meta, tiles, depth):
@@ -143,12 +143,12 @@
     return pl.pallas_call(
         functools.partial(order_kernel, depth, len(tiles)),
         out_shape=jax.ShapeDtypeStruct((2 * height, GROUP * depth), jnp.bfloat16),
-        in_specs=[smem, vmem] + [pl.BlockSpec(memory_space=pl.ANY)] * len(tiles),
+        in_specs=[smem, vmem] + [pl.BlockSpec(memory_space=pltpu.HBM)] * len(tiles),
         out_specs=vmem,
         scratch_shapes=[pltpu.VMEM((height, width), jnp.float32), pltpu.SemaphoreType.DMA],
         compiler_params=pltpu.CompilerParams(vmem_limit_bytes=32 << 20),
         cost_estimate=pl.CostEstimate(
-            flops=4 * height * width * GROUP * depth, bytes_accessed=4 * height * width, transcendentals=0
+            flops=40 * height * width * GROUP * depth, bytes_accessed=4 * height * width, transcendentals=0
         ),
         name="order_amplitudes",
     )(tasks, meta, *tiles)

time: 25.6 us -> 25.1 us (0.980)
  waiting for transfers between devices: 4.32 us -> 3.93 us
    ppermute x9, waiting for transfers between devices: 4.32 us -> 3.93 us  [swap(): lax.ppermute(values, axis, [(device, device ^ mask) for device in range(s...]
where the time goes in v3:
time: 25.1 us; the launch traced here: 24.9 us
  starting transfers between devices  12.5 us (50%)
  Pallas kernels  7.61 us (30%)
  waiting for transfers between devices  3.93 us (16%)
  loops' own time  0.68 us (3%)
    ppermute x9, starting transfers between devices, swap(): lax.ppermute(values, axis, [(device, device ^ mask) for device in range(s...  12.5 us
    ppermute x9, waiting for transfers between devices, swap(): lax.ppermute(values, axis, [(device, device ^ mask) for device in range(s...  3.93 us
    pallas_call x1, Pallas kernels, ladder(): pl.pallas_call(functools.partial(ladder_kernel, depth, masks, len(pieces)...  2.69 us
    pallas_call x1, Pallas kernels, order(): pl.pallas_call(functools.partial(order_kernel, depth, len(tiles)), out_sh...  2.29 us
    pallas_call x1, Pallas kernels, count(): pl.pallas_call(functools.partial(count_kernel, width), out_shape=jax.Shap...  1.4 us
    pallas_call x1, Pallas kernels, prep(): pl.pallas_call(functools.partial(prep_kernel, depth), out_shape=(jax.Shap...  1.23 us
    another operation x1, loops' own time, shards(): lax.while_loop(lambda state: state[0][0] < most[0], lambda state: (state[...  0.68 us
  transfers between devices with their start and end apart: 9, of which 4 were waited for; matrix products, arithmetic and copies ran while one was open for 0% of the time, Pallas kernels for 20%

profile of v3, /device:TPU:0, one launch (start us, length us, event | category | flops | bytes accessed | tf_op | source)
XLA Modules:
  0.0 24.9 jit_solution(5305874258437784030)
XLA Ops:
  0.0 0.0 copy-start.4
  0.0 0.0 copy-start
  0.0 0.0 copy-start.2
  0.0 0.0 copy-start.3
  0.0 0.0 copy-start.5
  0.0 0.0 copy-start.1
  0.0 3.0 %collective-permute-start.8 = (f32[128,1,1024]{2,1,0:T(1,128)}, f32[128,1,1024]{2,1,0:T(1,128)}, u32[]{:S(2)}, u32[]{:S(2)}) collective-permute-start(f32[128,1,1024]{2,1,0:T(1,128)} %refs_2_), channel_id=1, source_target_pairs={{0,2},{1,3},{2,0},{3,1},{4,6},{5,7},{6,4},{7,5},{8,10},{9,11},{10,... | collective-permute-start | bytes 1572872 | tf_op jit(solution)/shard_map/ppermute | solution.py:210
  3.1 0.0 collective-permute-start.7
  3.1 0.0 copy-done.4
  3.1 0.1 copy.7.pairs_ref
  3.2 0.0 copy-done
  3.2 0.0 copy-done.2
  3.2 0.0 copy-done.3
  3.2 1.2 %compact.3 = (f32[176,128]{1,0:T(8,128)S(1)}, s32[8,1024]{1,0:T(8,128)S(1)}) custom-call(s32[1]{0:T(128)} %constant.6.clone.1.first_ref, s32[4]{0:T(128)S(1)} %copy-done.3, s32[4,2]{1,0:T(4,128)S(1)} %copy.7.pairs_ref, s32[19,32]{1,0:T(8,128)S(1)} %copy-done.2, f32[128,1024]{1,0:T(8,128)S(1)} %bitcast.3), custom_call_target="tpu_custom_call" | custom-call | flops 92274688 | bytes 524288 | tf_op jit(solution)/shard_map/compact/pallas_call | solution.py:87
  4.4 2.6 %collective-permute-start.9 = (f32[176,128]{1,0:T(8,128)S(1)}, f32[176,128]{1,0:T(8,128)S(1)}, u32[]{:S(2)}, u32[]{:S(2)}) collective-permute-start(f32[176,128]{1,0:T(8,128)S(1)} %get-tuple-element.101.refs_0_), channel_id=1, source_target_pairs={{0,16},{4,20},{8,24},{12,28},{16,0},{20,4},{24,8},{28,12},{1,17},{... | collective-permute-start | bytes 270344 | tf_op jit(solution)/shard_map/ppermute | solution.py:210
  7.1 1.6 %collective-permute-start.10 = (f32[176,128]{1,0:T(8,128)S(1)}, f32[176,128]{1,0:T(8,128)S(1)}, u32[]{:S(2)}, u32[]{:S(2)}) collective-permute-start(f32[176,128]{1,0:T(8,128)S(1)} %get-tuple-element.101.refs_0_), channel_id=1, source_target_pairs={{0,8},{4,12},{8,0},{12,4},{16,24},{20,28},{24,16},{28,20},{1,9},{5... | collective-permute-start | bytes 270344 | tf_op jit(solution)/shard_map/ppermute | solution.py:210
  8.6 1.4 %count.1 = s32[1]{0:T(128)} custom-call(s32[4]{0:T(128)S(1)} %copy-done.3, s32[4,2]{1,0:T(4,128)S(1)} %copy.7.pairs_ref, s32[19,32]{1,0:T(8,128)S(1)} %copy-done.2), custom_call_target="tpu_custom_call" | custom-call | tf_op jit(solution)/shard_map/count/pallas_call | solution.py:114
  10.0 1.6 %collective-permute-start.11 = (f32[176,128]{1,0:T(8,128)S(1)}, f32[176,128]{1,0:T(8,128)S(1)}, u32[]{:S(2)}, u32[]{:S(2)}) collective-permute-start(f32[176,128]{1,0:T(8,128)S(1)} %get-tuple-element.101.refs_0_), channel_id=1, source_target_pairs={{0,4},{4,0},{8,12},{12,8},{16,20},{20,16},{24,28},{28,24},{1,5},{5... | collective-permute-start | bytes 270344 | tf_op jit(solution)/shard_map/ppermute | solution.py:210
  11.6 0.8 %collective-permute-done.9.refs_1_ = f32[176,128]{1,0:T(8,128)S(1)} collective-permute-done((f32[176,128]{1,0:T(8,128)S(1)}, f32[176,128]{1,0:T(8,128)S(1)}, u32[]{:S(2)}, u32[]{:S(2)}) %collective-permute-start.9) | collective-permute-done | bytes 90144 | tf_op jit(solution)/shard_map/ppermute | solution.py:210
  12.4 0.6 %collective-permute-start.13 = (f32[176,128]{1,0:T(8,128)S(1)}, f32[176,128]{1,0:T(8,128)S(1)}, u32[]{:S(2)}, u32[]{:S(2)}) collective-permute-start(f32[176,128]{1,0:T(8,128)S(1)} %collective-permute-done.9.refs_1_), channel_id=1, source_target_pairs={{0,8},{4,12},{8,0},{12,4},{16,24},{20,28},{24,16},{28,20},{1,9},{5... | collective-permute-start | bytes 270344 | tf_op jit(solution)/shard_map/ppermute | solution.py:210
  13.0 0.0 collective-permute-done.10.refs_2_
  13.0 1.6 %collective-permute-start.14 = (f32[352,128]{1,0:T(8,128)S(1)}, f32[352,128]{1,0:T(8,128)S(1)}, u32[]{:S(2)}, u32[]{:S(2)}) collective-permute-start(f32[352,128]{1,0:T(8,128)S(1)} %pad_maximum_fusion.1), channel_id=1, source_target_pairs={{0,4},{4,0},{8,12},{12,8},{16,20},{20,16},{24,28},{28,24},{1,5},{5... | collective-permute-start | bytes 540680 | tf_op jit(solution)/shard_map/ppermute | solution.py:210
  14.6 0.0 collective-permute-done.11.refs_4_
  14.6 0.7 %collective-permute-done.8.refs_4_ = f32[128,1,1024]{2,1,0:T(1,128)} collective-permute-done((f32[128,1,1024]{2,1,0:T(1,128)}, f32[128,1,1024]{2,1,0:T(1,128)}, u32[]{:S(2)}, u32[]{:S(2)}) %collective-permute-start.8) | collective-permute-done | bytes 524320 | tf_op jit(solution)/shard_map/ppermute | solution.py:210
  15.3 0.0 collective-permute-start.12
  15.3 1.6 %collective-permute-done.13.refs_3_ = f32[176,128]{1,0:T(8,128)S(1)} collective-permute-done((f32[176,128]{1,0:T(8,128)S(1)}, f32[176,128]{1,0:T(8,128)S(1)}, u32[]{:S(2)}, u32[]{:S(2)}) %collective-permute-start.13) | collective-permute-done | bytes 90144 | tf_op jit(solution)/shard_map/ppermute | solution.py:210
  17.0 0.0 collective-permute-done.7.refs_3_
  17.0 0.0 copy-done.5
  17.0 0.0 copy-done.1
  17.0 0.7 %while.11 = (s32[1]{0:T(128)}, f32[128,1,1024]{2,1,0:T(1,128)S(1)}, s32[1]{0:T(128)}, s32[4]{0:T(128)S(1)}, s32[4,2]{1,0:T(4,128)S(1)}, /*index=5*/s32[19,32]{1,...) while((s32[1]{0:T(128)}, f32[128,1,1024]{2,1,0:T(1,128)S(1)}, ...), condition=%wide.region_1.0_spmd, body=%wide.region_0.0_spmd | while | flops 8581591040 | bytes 8126853 | solution.py:265
  17.7 1.6 %collective-permute-start.15 = (f32[176,128]{1,0:T(8,128)S(1)}, f32[176,128]{1,0:T(8,128)S(1)}, u32[]{:S(2)}, u32[]{:S(2)}) collective-permute-start(f32[176,128]{1,0:T(8,128)S(1)} %collective-permute-done.13.refs_3_), channel_id=1, source_target_pairs={{0,4},{4,0},{8,12},{12,8},{16,20},{20,16},{24,28},{28,24},{1,5},{5... | collective-permute-start | bytes 270344 | tf_op jit(solution)/shard_map/ppermute | solution.py:210
  19.2 0.0 collective-permute-done.12.refs_5_
  19.2 2.3 %order_amplitudes.2.amps_ref = bf16[256,1408]{1,0:T(8,128)(2,1)S(1)} custom-call(s32[4]{0:T(128)S(1)} %get-tuple-element.258, s32[8,1024]{1,0:T(8,128)S(1)} %get-tuple-element.100.refs_1_.meta_ref, f32[128,1,1024]{2,1,0:T(1,128)S(1)} %get-tuple-element.261, f32[128,1,1024]{2,1,0:T(1,128)S(1)} %get-tuple-element.263, ...), custom_call_target="tpu_custom_call" | custom-call | flops 7381975040 | bytes 524288 | tf_op jit(solution)/shard_map/order_amplitudes/pallas_call | solution.py:143
  21.5 0.0 collective-permute-done.14.refs_5_
  21.5 0.7 %collective-permute-done.15.refs_6_ = f32[176,128]{1,0:T(8,128)S(1)} collective-permute-done((f32[176,128]{1,0:T(8,128)S(1)}, f32[176,128]{1,0:T(8,128)S(1)}, u32[]{:S(2)}, u32[]{:S(2)}) %collective-permute-start.15) | collective-permute-done | bytes 90144 | tf_op jit(solution)/shard_map/ppermute | solution.py:210
  22.3 2.7 %ladder.3 = f32[128,1,1024]{2,1,0:T(1,128)} custom-call(s32[8,1024]{1,0:T(8,128)S(1)} %get-tuple-element.100.refs_1_.meta_ref, bf16[256,1408]{1,0:T(8,128)(2,1)S(1)} %order_amplitudes.2.amps_ref, f32[176,128]{1,0:T(8,128)S(1)} %get-tuple-element.101.refs_0_, f32[176,128]{1,0:T(8,128)S(1)} %collective-permute-done.9.refs_1_, ...), custom_call_target="tpu_custom_call" | custom-call | flops 1107296256 | bytes 1048576 | tf_op jit(solution)/shard_map/ladder/pallas_call | solution.py:194
  (1 shorter events, 0.0 us)
Async XLA Ops:
  0.0 3.1 %copy-start.4 = (s32[4,2]{0,1:T(2,128)S(1)}, s32[4,2]{0,1:T(2,128)}, u32[]{:S(2)}) copy-start(s32[4,2]{0,1:T(2,128)} %param.12) | copy-start | bytes 100
  0.0 3.2 %copy-start = (f32[1,128,1024]{2,1,0:T(8,128)S(1)}, f32[1,128,1024]{2,1,0:T(8,128)}, u32[]{:S(2)}) copy-start(f32[1,128,1024]{2,1,0:T(8,128)} %param.10) | copy-start | bytes 1572868
  0.0 3.2 %copy-start.2 = (s32[19,32]{1,0:T(8,128)S(1)}, s32[19,32]{1,0:T(8,128)}, u32[]{:S(2)}) copy-start(s32[19,32]{1,0:T(8,128)} %irreps_ref.3) | copy-start | bytes 7300
  0.0 3.2 %copy-start.3 = (s32[4]{0:T(128)S(1)}, s32[4]{0:T(128)}, u32[]{:S(2)}) copy-start(s32[4]{0:T(128)} %refs_0_.1) | copy-start | bytes 52
  0.0 17.0 %copy-start.5 = (f32[128,1,1024]{2,1,0:T(1,128)S(1)}, f32[128,1,1024]{2,1,0:T(1,128)}, u32[]{:S(2)}) copy-start(f32[128,1,1024]{2,1,0:T(1,128)} %refs_2_) | copy-start | bytes 1572868
  0.0 17.0 %copy-start.1 = (f32[128,1,1024]{2,1,0:T(1,128)S(1)}, f32[128,1,1024]{2,1,0:T(1,128)}, u32[]{:S(2)}) copy-start(f32[128,1,1024]{2,1,0:T(1,128)} %param.9) | copy-start | bytes 1572868
  0.0 15.3 %collective-permute-start.8 = (f32[128,1,1024]{2,1,0:T(1,128)}, f32[128,1,1024]{2,1,0:T(1,128)}, u32[]{:S(2)}, u32[]{:S(2)}) collective-permute-start(f32[128,1,1024]{2,1,0:T(1,128)} %refs_2_), channel_id=1, source_target_pairs={{0,2},{1,3},{2,0},{3,1},{4,6},{5,7},{6,4},{7,5},{8,10},{9,11},{10,... | collective-permute-start | bytes 1572872 | tf_op jit(solution)/shard_map/ppermute | solution.py:210
  3.1 13.9 %collective-permute-start.7 = (f32[128,1,1024]{2,1,0:T(1,128)}, f32[128,1,1024]{2,1,0:T(1,128)S(1)}, u32[]{:S(2)}, u32[]{:S(2)}) collective-permute-start(f32[128,1,1024]{2,1,0:T(1,128)} %refs_2_), channel_id=1, source_target_pairs={{0,1},{1,0},{2,3},{3,2},{4,5},{5,4},{6,7},{7,6},{8,9},{9,8},{10,11... | collective-permute-start | bytes 1572872 | tf_op jit(solution)/shard_map/ppermute | solution.py:210
  4.4 8.0 %collective-permute-start.9 = (f32[176,128]{1,0:T(8,128)S(1)}, f32[176,128]{1,0:T(8,128)S(1)}, u32[]{:S(2)}, u32[]{:S(2)}) collective-permute-start(f32[176,128]{1,0:T(8,128)S(1)} %get-tuple-element.101.refs_0_), channel_id=1, source_target_pairs={{0,16},{4,20},{8,24},{12,28},{16,0},{20,4},{24,8},{28,12},{1,17},{... | collective-permute-start | bytes 270344 | tf_op jit(solution)/shard_map/ppermute | solution.py:210
  7.1 6.0 %collective-permute-start.10 = (f32[176,128]{1,0:T(8,128)S(1)}, f32[176,128]{1,0:T(8,128)S(1)}, u32[]{:S(2)}, u32[]{:S(2)}) collective-permute-start(f32[176,128]{1,0:T(8,128)S(1)} %get-tuple-element.101.refs_0_), channel_id=1, source_target_pairs={{0,8},{4,12},{8,0},{12,4},{16,24},{20,28},{24,16},{28,20},{1,9},{5... | collective-permute-start | bytes 270344 | tf_op jit(solution)/shard_map/ppermute | solution.py:210
  10.0 4.6 %collective-permute-start.11 = (f32[176,128]{1,0:T(8,128)S(1)}, f32[176,128]{1,0:T(8,128)S(1)}, u32[]{:S(2)}, u32[]{:S(2)}) collective-permute-start(f32[176,128]{1,0:T(8,128)S(1)} %get-tuple-element.101.refs_0_), channel_id=1, source_target_pairs={{0,4},{4,0},{8,12},{12,8},{16,20},{20,16},{24,28},{28,24},{1,5},{5... | collective-permute-start | bytes 270344 | tf_op jit(solution)/shard_map/ppermute | solution.py:210
  12.4 4.5 %collective-permute-start.13 = (f32[176,128]{1,0:T(8,128)S(1)}, f32[176,128]{1,0:T(8,128)S(1)}, u32[]{:S(2)}, u32[]{:S(2)}) collective-permute-start(f32[176,128]{1,0:T(8,128)S(1)} %collective-permute-done.9.refs_1_), channel_id=1, source_target_pairs={{0,8},{4,12},{8,0},{12,4},{16,24},{20,28},{24,16},{28,20},{1,9},{5... | collective-permute-start | bytes 270344 | tf_op jit(solution)/shard_map/ppermute | solution.py:210
  13.0 8.5 %collective-permute-start.14 = (f32[352,128]{1,0:T(8,128)S(1)}, f32[352,128]{1,0:T(8,128)S(1)}, u32[]{:S(2)}, u32[]{:S(2)}) collective-permute-start(f32[352,128]{1,0:T(8,128)S(1)} %pad_maximum_fusion.1), channel_id=1, source_target_pairs={{0,4},{4,0},{8,12},{12,8},{16,20},{20,16},{24,28},{28,24},{1,5},{5... | collective-permute-start | bytes 540680 | tf_op jit(solution)/shard_map/ppermute | solution.py:210
  15.3 3.9 %collective-permute-start.12 = (f32[128,1,1024]{2,1,0:T(1,128)}, f32[128,1,1024]{2,1,0:T(1,128)S(1)}, u32[]{:S(2)}, u32[]{:S(2)}) collective-permute-start(f32[128,1,1024]{2,1,0:T(1,128)} %collective-permute-done.8.refs_4_), channel_id=1, source_target_pairs={{0,1},{1,0},{2,3},{3,2},{4,5},{5,4},{6,7},{7,6},{8,9},{9,8},{10,11... | collective-permute-start | bytes 1572872 | tf_op jit(solution)/shard_map/ppermute | solution.py:210
  17.7 4.6 %collective-permute-start.15 = (f32[176,128]{1,0:T(8,128)S(1)}, f32[176,128]{1,0:T(8,128)S(1)}, u32[]{:S(2)}, u32[]{:S(2)}) collective-permute-start(f32[176,128]{1,0:T(8,128)S(1)} %collective-permute-done.13.refs_3_), channel_id=1, source_target_pairs={{0,4},{4,0},{8,12},{12,8},{16,20},{20,16},{24,28},{28,24},{1,5},{5... | collective-permute-start | bytes 270344 | tf_op jit(solution)/shard_map/ppermute | solution.py:210

commit v4 on v3

--- a/solution.py
+++ b/solution.py
@@ -155,55 +155,46 @@
 
 
 def ladder_kernel(depth, masks, count, meta_ref, amps_ref, *refs):
-    pieces, base_ref, (out_ref, held, sems) = refs[:count], refs[count], refs[-3:]
+    pieces, (base_ref, out_ref, held, load_sem, store_sem) = refs[:count], refs[count:]
     block = lax.axis_index("occ")
-    height = held.shape[0]
+    height, width = held.shape
     size = pieces[0].shape[1]
     pieces = [piece.at[at : at + depth] for piece in pieces for at in range(0, piece.shape[0], depth)]
-    places = [pl.ds(pl.multiple_of(jnp.bitwise_xor(block, mask) * size, LANES), size) for mask in masks]
-    loads = [
-        pltpu.make_async_copy(base_ref.at[:, 0, place], held.at[:, n * size : (n + 1) * size], sems.at[n])
-        for n, place in enumerate(places)
-    ]
-    for load in loads:
-        load.start()
+    if size == width:
+        places = [pl.ds(0, size)]
+    else:
+        places = [pl.ds(pl.multiple_of(jnp.bitwise_xor(block, mask) * size, LANES), size) for mask in masks]
+    load = pltpu.make_async_copy(base_ref.at[:, 0, :], held, load_sem)
+    load.start()
     high, low = split(jnp.concatenate([piece[...] for piece in pieces], axis=1))
     irrep = jnp.concatenate([meta_ref[1:2, place] for place in places], axis=1)
     zero = jnp.zeros((), jnp.bfloat16)
     blocks = lambda values: jnp.concatenate([jnp.where(irrep == g, values, zero) for g in range(GROUP)], axis=0)
     both = dot(amps_ref[...], blocks(high), NN)
     ladder = both[:height] + both[height:] + dot(amps_ref[:height], blocks(low), NN)
-    for load in loads:
-        load.wait()
-    held[...] += ladder
-    stores = [
-        pltpu.make_async_copy(held.at[:, n * size : (n + 1) * size], out_ref.at[:, 0, place], sems.at[n])
-        for n, place in enumerate(places)
-    ]
-    for store in stores:
-        store.start()
-    for store in stores:
-        store.wait()
-
-
-def ladder(meta, amps, masks, pieces, base, out, depth):
-    into = () if out is None else (out,)
-    height, size = base.shape[0], pieces[0].shape[1]
+    load.wait()
+    for n, place in enumerate(places):
+        held[:, place] += ladder[:, n * size : (n + 1) * size]
+    store = pltpu.make_async_copy(held, out_ref.at[:, 0, :], store_sem)
+    store.start()
+    store.wait()
+
+
+def ladder(meta, amps, masks, pieces, base, depth):
+    height, _, width = base.shape
     vmem, hbm = pl.BlockSpec(memory_space=pltpu.VMEM), pl.BlockSpec(memory_space=pl.ANY)
-    columns = size * len(masks)
     return pl.pallas_call(
         functools.partial(ladder_kernel, depth, masks, len(pieces)),
         out_shape=jax.ShapeDtypeStruct(base.shape, base.dtype),
-        in_specs=[vmem, vmem] + [vmem] * len(pieces) + [hbm] * (1 + len(into)),
+        in_specs=[vmem, vmem] + [vmem] * len(pieces) + [hbm],
         out_specs=hbm,
-        scratch_shapes=[pltpu.VMEM((height, columns), jnp.float32), pltpu.SemaphoreType.DMA((len(masks),))],
-        input_output_aliases={3 + len(pieces): 0} if into else {},
+        scratch_shapes=[pltpu.VMEM((height, width), jnp.float32), pltpu.SemaphoreType.DMA, pltpu.SemaphoreType.DMA],
         compiler_params=pltpu.CompilerParams(vmem_limit_bytes=48 << 20),
         cost_estimate=pl.CostEstimate(
-            flops=6 * height * columns * GROUP * depth, bytes_accessed=8 * height * columns, transcendentals=0
+            flops=6 * height * width * GROUP * depth, bytes_accessed=8 * height * width, transcendentals=0
         ),
         name="ladder",
-    )(meta, amps, *pieces, base, *into)
+    )(meta, amps, *pieces, base)
 
 
 def swap(values, axis, size, mask):
@@ -259,7 +250,7 @@
             tiles = other_swaps(tiles, vir_size)
         tiles, base = lax.optimization_barrier((tiles, base))
         ordered = order(tasks, meta, tiles, depth)
-        return ladder(meta, ordered, sum(blocks, ()), list(blocks.values()), base, None, depth)
+        return ladder(meta, ordered, sum(blocks, ()), list(blocks.values()), base, depth)
 
     most = count(tasks, pair_tiles, irreps, width)
     rest = lax.while_loop(

time: 25.1 us -> 25.1 us (level)
  no operation moved by 1% of the time
where the time goes in v4:
time: 25.1 us; the launch traced here: 24.9 us
  starting transfers between devices  12.5 us (50%)
  Pallas kernels  7.59 us (30%)
  waiting for transfers between devices  3.93 us (16%)
  loops' own time  0.68 us (3%)
    ppermute x9, starting transfers between devices, swap(): lax.ppermute(values, axis, [(device, device ^ mask) for device in range(s...  12.5 us
    ppermute x9, waiting for transfers between devices, swap(): lax.ppermute(values, axis, [(device, device ^ mask) for device in range(s...  3.93 us
    pallas_call x1, Pallas kernels, ladder(): pl.pallas_call(functools.partial(ladder_kernel, depth, masks, len(pieces)...  2.68 us
    pallas_call x1, Pallas kernels, order(): pl.pallas_call(functools.partial(order_kernel, depth, len(tiles)), out_sh...  2.29 us
    pallas_call x1, Pallas kernels, count(): pl.pallas_call(functools.partial(count_kernel, width), out_shape=jax.Shap...  1.4 us
    pallas_call x1, Pallas kernels, prep(): pl.pallas_call(functools.partial(prep_kernel, depth), out_shape=(jax.Shap...  1.23 us
    another operation x1, loops' own time, shards(): lax.while_loop(lambda state: state[0][0] < most[0], lambda state: (state[...  0.68 us
  transfers between devices with their start and end apart: 9, of which 4 were waited for; matrix products, arithmetic and copies ran while one was open for 0% of the time, Pallas kernels for 20%

profile of v4, /device:TPU:0, one launch (start us, length us, event | category | flops | bytes accessed | tf_op | source)
XLA Modules:
  0.0 24.9 jit_solution(7600741636121787171)
XLA Ops:
  0.0 0.0 copy-start.4
  0.0 0.0 copy-start
  0.0 0.0 copy-start.2
  0.0 0.0 copy-start.3
  0.0 0.0 copy-start.5
  0.0 0.0 copy-start.1
  0.0 3.0 %collective-permute-start.8 = (f32[128,1,1024]{2,1,0:T(1,128)}, f32[128,1,1024]{2,1,0:T(1,128)}, u32[]{:S(2)}, u32[]{:S(2)}) collective-permute-start(f32[128,1,1024]{2,1,0:T(1,128)} %refs_2_), channel_id=1, source_target_pairs={{0,2},{1,3},{2,0},{3,1},{4,6},{5,7},{6,4},{7,5},{8,10},{9,11},{10,... | collective-permute-start | bytes 1572872 | tf_op jit(solution)/shard_map/ppermute | solution.py:201
  3.1 0.0 collective-permute-start.7
  3.1 0.0 copy-done.4
  3.1 0.1 copy.7.pairs_ref
  3.2 0.0 copy-done
  3.2 0.0 copy-done.2
  3.2 0.0 copy-done.3
  3.2 1.2 %compact.3 = (f32[176,128]{1,0:T(8,128)S(1)}, s32[8,1024]{1,0:T(8,128)S(1)}) custom-call(s32[1]{0:T(128)} %constant.6.clone.1.first_ref, s32[4]{0:T(128)S(1)} %copy-done.3, s32[4,2]{1,0:T(4,128)S(1)} %copy.7.pairs_ref, s32[19,32]{1,0:T(8,128)S(1)} %copy-done.2, f32[128,1024]{1,0:T(8,128)S(1)} %bitcast.3), custom_call_target="tpu_custom_call" | custom-call | flops 92274688 | bytes 524288 | tf_op jit(solution)/shard_map/compact/pallas_call | solution.py:87
  4.4 2.6 %collective-permute-start.9 = (f32[176,128]{1,0:T(8,128)S(1)}, f32[176,128]{1,0:T(8,128)S(1)}, u32[]{:S(2)}, u32[]{:S(2)}) collective-permute-start(f32[176,128]{1,0:T(8,128)S(1)} %get-tuple-element.101.refs_0_), channel_id=1, source_target_pairs={{0,16},{4,20},{8,24},{12,28},{16,0},{20,4},{24,8},{28,12},{1,17},{... | collective-permute-start | bytes 270344 | tf_op jit(solution)/shard_map/ppermute | solution.py:201
  7.1 1.6 %collective-permute-start.10 = (f32[176,128]{1,0:T(8,128)S(1)}, f32[176,128]{1,0:T(8,128)S(1)}, u32[]{:S(2)}, u32[]{:S(2)}) collective-permute-start(f32[176,128]{1,0:T(8,128)S(1)} %get-tuple-element.101.refs_0_), channel_id=1, source_target_pairs={{0,8},{4,12},{8,0},{12,4},{16,24},{20,28},{24,16},{28,20},{1,9},{5... | collective-permute-start | bytes 270344 | tf_op jit(solution)/shard_map/ppermute | solution.py:201
  8.6 1.4 %count.1 = s32[1]{0:T(128)} custom-call(s32[4]{0:T(128)S(1)} %copy-done.3, s32[4,2]{1,0:T(4,128)S(1)} %copy.7.pairs_ref, s32[19,32]{1,0:T(8,128)S(1)} %copy-done.2), custom_call_target="tpu_custom_call" | custom-call | tf_op jit(solution)/shard_map/count/pallas_call | solution.py:114
  10.0 1.6 %collective-permute-start.11 = (f32[176,128]{1,0:T(8,128)S(1)}, f32[176,128]{1,0:T(8,128)S(1)}, u32[]{:S(2)}, u32[]{:S(2)}) collective-permute-start(f32[176,128]{1,0:T(8,128)S(1)} %get-tuple-element.101.refs_0_), channel_id=1, source_target_pairs={{0,4},{4,0},{8,12},{12,8},{16,20},{20,16},{24,28},{28,24},{1,5},{5... | collective-permute-start | bytes 270344 | tf_op jit(solution)/shard_map/ppermute | solution.py:201
  11.6 0.8 %collective-permute-done.9.refs_1_ = f32[176,128]{1,0:T(8,128)S(1)} collective-permute-done((f32[176,128]{1,0:T(8,128)S(1)}, f32[176,128]{1,0:T(8,128)S(1)}, u32[]{:S(2)}, u32[]{:S(2)}) %collective-permute-start.9) | collective-permute-done | bytes 90144 | tf_op jit(solution)/shard_map/ppermute | solution.py:201
  12.4 0.6 %collective-permute-start.13 = (f32[176,128]{1,0:T(8,128)S(1)}, f32[176,128]{1,0:T(8,128)S(1)}, u32[]{:S(2)}, u32[]{:S(2)}) collective-permute-start(f32[176,128]{1,0:T(8,128)S(1)} %collective-permute-done.9.refs_1_), channel_id=1, source_target_pairs={{0,8},{4,12},{8,0},{12,4},{16,24},{20,28},{24,16},{28,20},{1,9},{5... | collective-permute-start | bytes 270344 | tf_op jit(solution)/shard_map/ppermute | solution.py:201
  13.0 0.0 collective-permute-done.10.refs_2_
  13.0 1.6 %collective-permute-start.14 = (f32[352,128]{1,0:T(8,128)S(1)}, f32[352,128]{1,0:T(8,128)S(1)}, u32[]{:S(2)}, u32[]{:S(2)}) collective-permute-start(f32[352,128]{1,0:T(8,128)S(1)} %pad_maximum_fusion.1), channel_id=1, source_target_pairs={{0,4},{4,0},{8,12},{12,8},{16,20},{20,16},{24,28},{28,24},{1,5},{5... | collective-permute-start | bytes 540680 | tf_op jit(solution)/shard_map/ppermute | solution.py:201
  14.6 0.0 collective-permute-done.11.refs_4_
  14.6 0.7 %collective-permute-done.8.refs_4_ = f32[128,1,1024]{2,1,0:T(1,128)} collective-permute-done((f32[128,1,1024]{2,1,0:T(1,128)}, f32[128,1,1024]{2,1,0:T(1,128)}, u32[]{:S(2)}, u32[]{:S(2)}) %collective-permute-start.8) | collective-permute-done | bytes 524320 | tf_op jit(solution)/shard_map/ppermute | solution.py:201
  15.3 0.0 collective-permute-start.12
  15.3 1.6 %collective-permute-done.13.refs_3_ = f32[176,128]{1,0:T(8,128)S(1)} collective-permute-done((f32[176,128]{1,0:T(8,128)S(1)}, f32[176,128]{1,0:T(8,128)S(1)}, u32[]{:S(2)}, u32[]{:S(2)}) %collective-permute-start.13) | collective-permute-done | bytes 90144 | tf_op jit(solution)/shard_map/ppermute | solution.py:201
  17.0 0.0 collective-permute-done.7.refs_3_
  17.0 0.0 copy-done.5
  17.0 0.0 copy-done.1
  17.0 0.7 %while.11 = (s32[1]{0:T(128)}, f32[128,1,1024]{2,1,0:T(1,128)S(1)}, s32[1]{0:T(128)}, s32[4]{0:T(128)S(1)}, s32[4,2]{1,0:T(4,128)S(1)}, /*index=5*/s32[19,32]{1,...) while((s32[1]{0:T(128)}, f32[128,1,1024]{2,1,0:T(1,128)S(1)}, ...), condition=%wide.region_1.0_spmd, body=%wide.region_0.0_spmd | while | flops 8581591040 | bytes 8126853 | solution.py:256
  17.7 1.6 %collective-permute-start.15 = (f32[176,128]{1,0:T(8,128)S(1)}, f32[176,128]{1,0:T(8,128)S(1)}, u32[]{:S(2)}, u32[]{:S(2)}) collective-permute-start(f32[176,128]{1,0:T(8,128)S(1)} %collective-permute-done.13.refs_3_), channel_id=1, source_target_pairs={{0,4},{4,0},{8,12},{12,8},{16,20},{20,16},{24,28},{28,24},{1,5},{5... | collective-permute-start | bytes 270344 | tf_op jit(solution)/shard_map/ppermute | solution.py:201
  19.2 0.0 collective-permute-done.12.refs_5_
  19.2 2.3 %order_amplitudes.2.amps_ref = bf16[256,1408]{1,0:T(8,128)(2,1)S(1)} custom-call(s32[4]{0:T(128)S(1)} %get-tuple-element.258, s32[8,1024]{1,0:T(8,128)S(1)} %get-tuple-element.100.refs_1_.meta_ref, f32[128,1,1024]{2,1,0:T(1,128)S(1)} %get-tuple-element.261, f32[128,1,1024]{2,1,0:T(1,128)S(1)} %get-tuple-element.263, ...), custom_call_target="tpu_custom_call" | custom-call | flops 7381975040 | bytes 524288 | tf_op jit(solution)/shard_map/order_amplitudes/pallas_call | solution.py:143
  21.5 0.0 collective-permute-done.14.refs_5_
  21.5 0.7 %collective-permute-done.15.refs_6_ = f32[176,128]{1,0:T(8,128)S(1)} collective-permute-done((f32[176,128]{1,0:T(8,128)S(1)}, f32[176,128]{1,0:T(8,128)S(1)}, u32[]{:S(2)}, u32[]{:S(2)}) %collective-permute-start.15) | collective-permute-done | bytes 90144 | tf_op jit(solution)/shard_map/ppermute | solution.py:201
  22.3 2.7 %ladder.3 = f32[128,1,1024]{2,1,0:T(1,128)} custom-call(s32[8,1024]{1,0:T(8,128)S(1)} %get-tuple-element.100.refs_1_.meta_ref, bf16[256,1408]{1,0:T(8,128)(2,1)S(1)} %order_amplitudes.2.amps_ref, f32[176,128]{1,0:T(8,128)S(1)} %get-tuple-element.101.refs_0_, f32[176,128]{1,0:T(8,128)S(1)} %collective-permute-done.9.refs_1_, ...), custom_call_target="tpu_custom_call" | custom-call | flops 1107296256 | bytes 1048576 | tf_op jit(solution)/shard_map/ladder/pallas_call | solution.py:186
  (1 shorter events, 0.0 us)
Async XLA Ops:
  0.0 3.1 %copy-start.4 = (s32[4,2]{0,1:T(2,128)S(1)}, s32[4,2]{0,1:T(2,128)}, u32[]{:S(2)}) copy-start(s32[4,2]{0,1:T(2,128)} %param.12) | copy-start | bytes 100
  0.0 3.2 %copy-start = (f32[1,128,1024]{2,1,0:T(8,128)S(1)}, f32[1,128,1024]{2,1,0:T(8,128)}, u32[]{:S(2)}) copy-start(f32[1,128,1024]{2,1,0:T(8,128)} %param.10) | copy-start | bytes 1572868
  0.0 3.2 %copy-start.2 = (s32[19,32]{1,0:T(8,128)S(1)}, s32[19,32]{1,0:T(8,128)}, u32[]{:S(2)}) copy-start(s32[19,32]{1,0:T(8,128)} %irreps_ref.3) | copy-start | bytes 7300
  0.0 3.2 %copy-start.3 = (s32[4]{0:T(128)S(1)}, s32[4]{0:T(128)}, u32[]{:S(2)}) copy-start(s32[4]{0:T(128)} %refs_0_.1) | copy-start | bytes 52
  0.0 17.0 %copy-start.5 = (f32[128,1,1024]{2,1,0:T(1,128)S(1)}, f32[128,1,1024]{2,1,0:T(1,128)}, u32[]{:S(2)}) copy-start(f32[128,1,1024]{2,1,0:T(1,128)} %refs_2_) | copy-start | bytes 1572868
  0.0 17.0 %copy-start.1 = (f32[128,1,1024]{2,1,0:T(1,128)S(1)}, f32[128,1,1024]{2,1,0:T(1,128)}, u32[]{:S(2)}) copy-start(f32[128,1,1024]{2,1,0:T(1,128)} %param.9) | copy-start | bytes 1572868
  0.0 15.3 %collective-permute-start.8 = (f32[128,1,1024]{2,1,0:T(1,128)}, f32[128,1,1024]{2,1,0:T(1,128)}, u32[]{:S(2)}, u32[]{:S(2)}) collective-permute-start(f32[128,1,1024]{2,1,0:T(1,128)} %refs_2_), channel_id=1, source_target_pairs={{0,2},{1,3},{2,0},{3,1},{4,6},{5,7},{6,4},{7,5},{8,10},{9,11},{10,... | collective-permute-start | bytes 1572872 | tf_op jit(solution)/shard_map/ppermute | solution.py:201
  3.1 13.9 %collective-permute-start.7 = (f32[128,1,1024]{2,1,0:T(1,128)}, f32[128,1,1024]{2,1,0:T(1,128)S(1)}, u32[]{:S(2)}, u32[]{:S(2)}) collective-permute-start(f32[128,1,1024]{2,1,0:T(1,128)} %refs_2_), channel_id=1, source_target_pairs={{0,1},{1,0},{2,3},{3,2},{4,5},{5,4},{6,7},{7,6},{8,9},{9,8},{10,11... | collective-permute-start | bytes 1572872 | tf_op jit(solution)/shard_map/ppermute | solution.py:201
  4.4 8.0 %collective-permute-start.9 = (f32[176,128]{1,0:T(8,128)S(1)}, f32[176,128]{1,0:T(8,128)S(1)}, u32[]{:S(2)}, u32[]{:S(2)}) collective-permute-start(f32[176,128]{1,0:T(8,128)S(1)} %get-tuple-element.101.refs_0_), channel_id=1, source_target_pairs={{0,16},{4,20},{8,24},{12,28},{16,0},{20,4},{24,8},{28,12},{1,17},{... | collective-permute-start | bytes 270344 | tf_op jit(solution)/shard_map/ppermute | solution.py:201
  7.1 6.0 %collective-permute-start.10 = (f32[176,128]{1,0:T(8,128)S(1)}, f32[176,128]{1,0:T(8,128)S(1)}, u32[]{:S(2)}, u32[]{:S(2)}) collective-permute-start(f32[176,128]{1,0:T(8,128)S(1)} %get-tuple-element.101.refs_0_), channel_id=1, source_target_pairs={{0,8},{4,12},{8,0},{12,4},{16,24},{20,28},{24,16},{28,20},{1,9},{5... | collective-permute-start | bytes 270344 | tf_op jit(solution)/shard_map/ppermute | solution.py:201
  10.0 4.6 %collective-permute-start.11 = (f32[176,128]{1,0:T(8,128)S(1)}, f32[176,128]{1,0:T(8,128)S(1)}, u32[]{:S(2)}, u32[]{:S(2)}) collective-permute-start(f32[176,128]{1,0:T(8,128)S(1)} %get-tuple-element.101.refs_0_), channel_id=1, source_target_pairs={{0,4},{4,0},{8,12},{12,8},{16,20},{20,16},{24,28},{28,24},{1,5},{5... | collective-permute-start | bytes 270344 | tf_op jit(solution)/shard_map/ppermute | solution.py:201
  12.4 4.5 %collective-permute-start.13 = (f32[176,128]{1,0:T(8,128)S(1)}, f32[176,128]{1,0:T(8,128)S(1)}, u32[]{:S(2)}, u32[]{:S(2)}) collective-permute-start(f32[176,128]{1,0:T(8,128)S(1)} %collective-permute-done.9.refs_1_), channel_id=1, source_target_pairs={{0,8},{4,12},{8,0},{12,4},{16,24},{20,28},{24,16},{28,20},{1,9},{5... | collective-permute-start | bytes 270344 | tf_op jit(solution)/shard_map/ppermute | solution.py:201
  13.0 8.5 %collective-permute-start.14 = (f32[352,128]{1,0:T(8,128)S(1)}, f32[352,128]{1,0:T(8,128)S(1)}, u32[]{:S(2)}, u32[]{:S(2)}) collective-permute-start(f32[352,128]{1,0:T(8,128)S(1)} %pad_maximum_fusion.1), channel_id=1, source_target_pairs={{0,4},{4,0},{8,12},{12,8},{16,20},{20,16},{24,28},{28,24},{1,5},{5... | collective-permute-start | bytes 540680 | tf_op jit(solution)/shard_map/ppermute | solution.py:201
  15.3 3.9 %collective-permute-start.12 = (f32[128,1,1024]{2,1,0:T(1,128)}, f32[128,1,1024]{2,1,0:T(1,128)S(1)}, u32[]{:S(2)}, u32[]{:S(2)}) collective-permute-start(f32[128,1,1024]{2,1,0:T(1,128)} %collective-permute-done.8.refs_4_), channel_id=1, source_target_pairs={{0,1},{1,0},{2,3},{3,2},{4,5},{5,4},{6,7},{7,6},{8,9},{9,8},{10,11... | collective-permute-start | bytes 1572872 | tf_op jit(solution)/shard_map/ppermute | solution.py:201
  17.7 4.6 %collective-permute-start.15 = (f32[176,128]{1,0:T(8,128)S(1)}, f32[176,128]{1,0:T(8,128)S(1)}, u32[]{:S(2)}, u32[]{:S(2)}) collective-permute-start(f32[176,128]{1,0:T(8,128)S(1)} %collective-permute-done.13.refs_3_), channel_id=1, source_target_pairs={{0,4},{4,0},{8,12},{12,8},{16,20},{20,16},{24,28},{28,24},{1,5},{5... | collective-permute-start | bytes 270344 | tf_op jit(solution)/shard_map/ppermute | solution.py:201

commit v5 on v4

--- a/solution.py
+++ b/solution.py
@@ -78,7 +78,8 @@
     live = jnp.bitwise_xor(outer, inner) == cd_irrep[:1]
     high, low = split(jnp.where(live, ints_ref[...], 0.0))
     pick = (iota((depth, width), 0) == rank).astype(jnp.bfloat16)
-    buf_ref[...] = dot(pick, high, NT) + dot(pick, low, NT)
+    both = dot(pick, jnp.concatenate([high, low], axis=0), NT)
+    buf_ref[...] = both[:, :height] + both[:, height:]
 
 
 def prep(first, tasks, pairs, irreps, ints, depth):

time: 25.1 us -> 25 us (level)
  transfers between devices with their start and end apart: 9 -> 9, of which waited for: 4 -> 4; matrix products, arithmetic and copies ran while one was open for 0% -> 0% of each run, Pallas kernels for 20% -> 19%
where the time goes in v5:
time: 25 us; the launch traced here: 24.9 us
  starting transfers between devices  12.5 us (50%)
  Pallas kernels  7.51 us (30%)
  waiting for transfers between devices  3.94 us (16%)
  loops' own time  0.68 us (3%)
    ppermute x9, starting transfers between devices, swap(): lax.ppermute(values, axis, [(device, device ^ mask) for device in range(s...  12.5 us
    ppermute x9, waiting for transfers between devices, swap(): lax.ppermute(values, axis, [(device, device ^ mask) for device in range(s...  3.94 us
    pallas_call x1, Pallas kernels, ladder(): pl.pallas_call(functools.partial(ladder_kernel, depth, masks, len(pieces)...  2.68 us
    pallas_call x1, Pallas kernels, order(): pl.pallas_call(functools.partial(order_kernel, depth, len(tiles)), out_sh...  2.29 us
    pallas_call x1, Pallas kernels, count(): pl.pallas_call(functools.partial(count_kernel, width), out_shape=jax.Shap...  1.4 us
    pallas_call x1, Pallas kernels, prep(): pl.pallas_call(functools.partial(prep_kernel, depth), out_shape=(jax.Shap...  1.15 us
    another operation x1, loops' own time, shards(): lax.while_loop(lambda state: state[0][0] < most[0], lambda state: (state[...  0.68 us
  transfers between devices with their start and end apart: 9, of which 4 were waited for; matrix products, arithmetic and copies ran while one was open for 0% of the time, Pallas kernels for 19%

profile of v5, /device:TPU:0, one launch (start us, length us, event | category | flops | bytes accessed | tf_op | source)
XLA Modules:
  0.0 24.9 jit_solution(3482026693826638929)
XLA Ops:
  0.0 0.0 copy-start.4
  0.0 0.0 copy-start
  0.0 0.0 copy-start.2
  0.0 0.0 copy-start.3
  0.0 0.0 copy-start.5
  0.0 0.0 copy-start.1
  0.0 3.0 %collective-permute-start.8 = (f32[128,1,1024]{2,1,0:T(1,128)}, f32[128,1,1024]{2,1,0:T(1,128)}, u32[]{:S(2)}, u32[]{:S(2)}) collective-permute-start(f32[128,1,1024]{2,1,0:T(1,128)} %refs_2_), channel_id=1, source_target_pairs={{0,2},{1,3},{2,0},{3,1},{4,6},{5,7},{6,4},{7,5},{8,10},{9,11},{10,... | collective-permute-start | bytes 1572872 | tf_op jit(solution)/shard_map/ppermute | solution.py:202
  3.1 0.0 collective-permute-start.7
  3.1 0.0 copy-done.4
  3.1 0.1 copy.7.pairs_ref
  3.2 0.0 copy-done
  3.2 0.0 copy-done.2
  3.2 0.0 copy-done.3
  3.2 1.1 %compact.3 = (f32[176,128]{1,0:T(8,128)S(1)}, s32[8,1024]{1,0:T(8,128)S(1)}) custom-call(s32[1]{0:T(128)} %constant.6.clone.1.first_ref, s32[4]{0:T(128)S(1)} %copy-done.3, s32[4,2]{1,0:T(4,128)S(1)} %copy.7.pairs_ref, s32[19,32]{1,0:T(8,128)S(1)} %copy-done.2, f32[128,1024]{1,0:T(8,128)S(1)} %bitcast.3), custom_call_target="tpu_custom_call" | custom-call | flops 92274688 | bytes 524288 | tf_op jit(solution)/shard_map/compact/pallas_call | solution.py:88
  4.3 2.7 %collective-permute-start.9 = (f32[176,128]{1,0:T(8,128)S(1)}, f32[176,128]{1,0:T(8,128)S(1)}, u32[]{:S(2)}, u32[]{:S(2)}) collective-permute-start(f32[176,128]{1,0:T(8,128)S(1)} %get-tuple-element.101.refs_0_), channel_id=1, source_target_pairs={{0,16},{4,20},{8,24},{12,28},{16,0},{20,4},{24,8},{28,12},{1,17},{... | collective-permute-start | bytes 270344 | tf_op jit(solution)/shard_map/ppermute | solution.py:202
  7.0 1.6 %collective-permute-start.10 = (f32[176,128]{1,0:T(8,128)S(1)}, f32[176,128]{1,0:T(8,128)S(1)}, u32[]{:S(2)}, u32[]{:S(2)}) collective-permute-start(f32[176,128]{1,0:T(8,128)S(1)} %get-tuple-element.101.refs_0_), channel_id=1, source_target_pairs={{0,8},{4,12},{8,0},{12,4},{16,24},{20,28},{24,16},{28,20},{1,9},{5... | collective-permute-start | bytes 270344 | tf_op jit(solution)/shard_map/ppermute | solution.py:202
  8.6 1.4 %count.1 = s32[1]{0:T(128)} custom-call(s32[4]{0:T(128)S(1)} %copy-done.3, s32[4,2]{1,0:T(4,128)S(1)} %copy.7.pairs_ref, s32[19,32]{1,0:T(8,128)S(1)} %copy-done.2), custom_call_target="tpu_custom_call" | custom-call | tf_op jit(solution)/shard_map/count/pallas_call | solution.py:115
  10.0 1.6 %collective-permute-start.11 = (f32[176,128]{1,0:T(8,128)S(1)}, f32[176,128]{1,0:T(8,128)S(1)}, u32[]{:S(2)}, u32[]{:S(2)}) collective-permute-start(f32[176,128]{1,0:T(8,128)S(1)} %get-tuple-element.101.refs_0_), channel_id=1, source_target_pairs={{0,4},{4,0},{8,12},{12,8},{16,20},{20,16},{24,28},{28,24},{1,5},{5... | collective-permute-start | bytes 270344 | tf_op jit(solution)/shard_map/ppermute | solution.py:202
  11.5 0.8 %collective-permute-done.9.refs_1_ = f32[176,128]{1,0:T(8,128)S(1)} collective-permute-done((f32[176,128]{1,0:T(8,128)S(1)}, f32[176,128]{1,0:T(8,128)S(1)}, u32[]{:S(2)}, u32[]{:S(2)}) %collective-permute-start.9) | collective-permute-done | bytes 90144 | tf_op jit(solution)/shard_map/ppermute | solution.py:202
  12.4 0.6 %collective-permute-start.13 = (f32[176,128]{1,0:T(8,128)S(1)}, f32[176,128]{1,0:T(8,128)S(1)}, u32[]{:S(2)}, u32[]{:S(2)}) collective-permute-start(f32[176,128]{1,0:T(8,128)S(1)} %collective-permute-done.9.refs_1_), channel_id=1, source_target_pairs={{0,8},{4,12},{8,0},{12,4},{16,24},{20,28},{24,16},{28,20},{1,9},{5... | collective-permute-start | bytes 270344 | tf_op jit(solution)/shard_map/ppermute | solution.py:202
  13.0 0.0 collective-permute-done.10.refs_2_
  13.0 1.6 %collective-permute-start.14 = (f32[352,128]{1,0:T(8,128)S(1)}, f32[352,128]{1,0:T(8,128)S(1)}, u32[]{:S(2)}, u32[]{:S(2)}) collective-permute-start(f32[352,128]{1,0:T(8,128)S(1)} %pad_maximum_fusion.1), channel_id=1, source_target_pairs={{0,4},{4,0},{8,12},{12,8},{16,20},{20,16},{24,28},{28,24},{1,5},{5... | collective-permute-start | bytes 540680 | tf_op jit(solution)/shard_map/ppermute | solution.py:202
  14.5 0.0 collective-permute-done.11.refs_4_
  14.6 0.7 %collective-permute-done.8.refs_4_ = f32[128,1,1024]{2,1,0:T(1,128)} collective-permute-done((f32[128,1,1024]{2,1,0:T(1,128)}, f32[128,1,1024]{2,1,0:T(1,128)}, u32[]{:S(2)}, u32[]{:S(2)}) %collective-permute-start.8) | collective-permute-done | bytes 524320 | tf_op jit(solution)/shard_map/ppermute | solution.py:202
  15.3 0.0 collective-permute-start.12
  15.3 1.6 %collective-permute-done.13.refs_3_ = f32[176,128]{1,0:T(8,128)S(1)} collective-permute-done((f32[176,128]{1,0:T(8,128)S(1)}, f32[176,128]{1,0:T(8,128)S(1)}, u32[]{:S(2)}, u32[]{:S(2)}) %collective-permute-start.13) | collective-permute-done | bytes 90144 | tf_op jit(solution)/shard_map/ppermute | solution.py:202
  16.9 0.0 collective-permute-done.7.refs_3_
  16.9 0.0 copy-done.5
  16.9 0.0 copy-done.1
  16.9 0.7 %while.11 = (s32[1]{0:T(128)}, f32[128,1,1024]{2,1,0:T(1,128)S(1)}, s32[1]{0:T(128)}, s32[4]{0:T(128)S(1)}, s32[4,2]{1,0:T(4,128)S(1)}, /*index=5*/s32[19,32]{1,...) while((s32[1]{0:T(128)}, f32[128,1,1024]{2,1,0:T(1,128)S(1)}, ...), condition=%wide.region_1.0_spmd, body=%wide.region_0.0_spmd | while | flops 8581591040 | bytes 8126853 | solution.py:257
  17.6 1.6 %collective-permute-start.15 = (f32[176,128]{1,0:T(8,128)S(1)}, f32[176,128]{1,0:T(8,128)S(1)}, u32[]{:S(2)}, u32[]{:S(2)}) collective-permute-start(f32[176,128]{1,0:T(8,128)S(1)} %collective-permute-done.13.refs_3_), channel_id=1, source_target_pairs={{0,4},{4,0},{8,12},{12,8},{16,20},{20,16},{24,28},{28,24},{1,5},{5... | collective-permute-start | bytes 270344 | tf_op jit(solution)/shard_map/ppermute | solution.py:202
  19.1 0.0 collective-permute-done.12.refs_5_
  19.2 2.3 %order_amplitudes.2.amps_ref = bf16[256,1408]{1,0:T(8,128)(2,1)S(1)} custom-call(s32[4]{0:T(128)S(1)} %get-tuple-element.258, s32[8,1024]{1,0:T(8,128)S(1)} %get-tuple-element.100.refs_1_.meta_ref, f32[128,1,1024]{2,1,0:T(1,128)S(1)} %get-tuple-element.261, f32[128,1,1024]{2,1,0:T(1,128)S(1)} %get-tuple-element.263, ...), custom_call_target="tpu_custom_call" | custom-call | flops 7381975040 | bytes 524288 | tf_op jit(solution)/shard_map/order_amplitudes/pallas_call | solution.py:144
  21.4 0.0 collective-permute-done.14.refs_5_
  21.5 0.7 %collective-permute-done.15.refs_6_ = f32[176,128]{1,0:T(8,128)S(1)} collective-permute-done((f32[176,128]{1,0:T(8,128)S(1)}, f32[176,128]{1,0:T(8,128)S(1)}, u32[]{:S(2)}, u32[]{:S(2)}) %collective-permute-start.15) | collective-permute-done | bytes 90144 | tf_op jit(solution)/shard_map/ppermute | solution.py:202
  22.2 2.7 %ladder.3 = f32[128,1,1024]{2,1,0:T(1,128)} custom-call(s32[8,1024]{1,0:T(8,128)S(1)} %get-tuple-element.100.refs_1_.meta_ref, bf16[256,1408]{1,0:T(8,128)(2,1)S(1)} %order_amplitudes.2.amps_ref, f32[176,128]{1,0:T(8,128)S(1)} %get-tuple-element.101.refs_0_, f32[176,128]{1,0:T(8,128)S(1)} %collective-permute-done.9.refs_1_, ...), custom_call_target="tpu_custom_call" | custom-call | flops 1107296256 | bytes 1048576 | tf_op jit(solution)/shard_map/ladder/pallas_call | solution.py:187
  (1 shorter events, 0.0 us)
Async XLA Ops:
  0.0 3.1 %copy-start.4 = (s32[4,2]{0,1:T(2,128)S(1)}, s32[4,2]{0,1:T(2,128)}, u32[]{:S(2)}) copy-start(s32[4,2]{0,1:T(2,128)} %param.12) | copy-start | bytes 100
  0.0 3.2 %copy-start = (f32[1,128,1024]{2,1,0:T(8,128)S(1)}, f32[1,128,1024]{2,1,0:T(8,128)}, u32[]{:S(2)}) copy-start(f32[1,128,1024]{2,1,0:T(8,128)} %param.10) | copy-start | bytes 1572868
  0.0 3.2 %copy-start.2 = (s32[19,32]{1,0:T(8,128)S(1)}, s32[19,32]{1,0:T(8,128)}, u32[]{:S(2)}) copy-start(s32[19,32]{1,0:T(8,128)} %irreps_ref.3) | copy-start | bytes 7300
  0.0 3.2 %copy-start.3 = (s32[4]{0:T(128)S(1)}, s32[4]{0:T(128)}, u32[]{:S(2)}) copy-start(s32[4]{0:T(128)} %refs_0_.1) | copy-start | bytes 52
  0.0 16.9 %copy-start.5 = (f32[128,1,1024]{2,1,0:T(1,128)S(1)}, f32[128,1,1024]{2,1,0:T(1,128)}, u32[]{:S(2)}) copy-start(f32[128,1,1024]{2,1,0:T(1,128)} %refs_2_) | copy-start | bytes 1572868
  0.0 16.9 %copy-start.1 = (f32[128,1,1024]{2,1,0:T(1,128)S(1)}, f32[128,1,1024]{2,1,0:T(1,128)}, u32[]{:S(2)}) copy-start(f32[128,1,1024]{2,1,0:T(1,128)} %param.9) | copy-start | bytes 1572868
  0.0 15.3 %collective-permute-start.8 = (f32[128,1,1024]{2,1,0:T(1,128)}, f32[128,1,1024]{2,1,0:T(1,128)}, u32[]{:S(2)}, u32[]{:S(2)}) collective-permute-start(f32[128,1,1024]{2,1,0:T(1,128)} %refs_2_), channel_id=1, source_target_pairs={{0,2},{1,3},{2,0},{3,1},{4,6},{5,7},{6,4},{7,5},{8,10},{9,11},{10,... | collective-permute-start | bytes 1572872 | tf_op jit(solution)/shard_map/ppermute | solution.py:202
  3.1 13.8 %collective-permute-start.7 = (f32[128,1,1024]{2,1,0:T(1,128)}, f32[128,1,1024]{2,1,0:T(1,128)S(1)}, u32[]{:S(2)}, u32[]{:S(2)}) collective-permute-start(f32[128,1,1024]{2,1,0:T(1,128)} %refs_2_), channel_id=1, source_target_pairs={{0,1},{1,0},{2,3},{3,2},{4,5},{5,4},{6,7},{7,6},{8,9},{9,8},{10,11... | collective-permute-start | bytes 1572872 | tf_op jit(solution)/shard_map/ppermute | solution.py:202
  4.3 8.0 %collective-permute-start.9 = (f32[176,128]{1,0:T(8,128)S(1)}, f32[176,128]{1,0:T(8,128)S(1)}, u32[]{:S(2)}, u32[]{:S(2)}) collective-permute-start(f32[176,128]{1,0:T(8,128)S(1)} %get-tuple-element.101.refs_0_), channel_id=1, source_target_pairs={{0,16},{4,20},{8,24},{12,28},{16,0},{20,4},{24,8},{28,12},{1,17},{... | collective-permute-start | bytes 270344 | tf_op jit(solution)/shard_map/ppermute | solution.py:202
  7.0 6.0 %collective-permute-start.10 = (f32[176,128]{1,0:T(8,128)S(1)}, f32[176,128]{1,0:T(8,128)S(1)}, u32[]{:S(2)}, u32[]{:S(2)}) collective-permute-start(f32[176,128]{1,0:T(8,128)S(1)} %get-tuple-element.101.refs_0_), channel_id=1, source_target_pairs={{0,8},{4,12},{8,0},{12,4},{16,24},{20,28},{24,16},{28,20},{1,9},{5... | collective-permute-start | bytes 270344 | tf_op jit(solution)/shard_map/ppermute | solution.py:202
  10.0 4.6 %collective-permute-start.11 = (f32[176,128]{1,0:T(8,128)S(1)}, f32[176,128]{1,0:T(8,128)S(1)}, u32[]{:S(2)}, u32[]{:S(2)}) collective-permute-start(f32[176,128]{1,0:T(8,128)S(1)} %get-tuple-element.101.refs_0_), channel_id=1, source_target_pairs={{0,4},{4,0},{8,12},{12,8},{16,20},{20,16},{24,28},{28,24},{1,5},{5... | collective-permute-start | bytes 270344 | tf_op jit(solution)/shard_map/ppermute | solution.py:202
  12.4 4.5 %collective-permute-start.13 = (f32[176,128]{1,0:T(8,128)S(1)}, f32[176,128]{1,0:T(8,128)S(1)}, u32[]{:S(2)}, u32[]{:S(2)}) collective-permute-start(f32[176,128]{1,0:T(8,128)S(1)} %collective-permute-done.9.refs_1_), channel_id=1, source_target_pairs={{0,8},{4,12},{8,0},{12,4},{16,24},{20,28},{24,16},{28,20},{1,9},{5... | collective-permute-start | bytes 270344 | tf_op jit(solution)/shard_map/ppermute | solution.py:202
  13.0 8.5 %collective-permute-start.14 = (f32[352,128]{1,0:T(8,128)S(1)}, f32[352,128]{1,0:T(8,128)S(1)}, u32[]{:S(2)}, u32[]{:S(2)}) collective-permute-start(f32[352,128]{1,0:T(8,128)S(1)} %pad_maximum_fusion.1), channel_id=1, source_target_pairs={{0,4},{4,0},{8,12},{12,8},{16,20},{20,16},{24,28},{28,24},{1,5},{5... | collective-permute-start | bytes 540680 | tf_op jit(solution)/shard_map/ppermute | solution.py:202
  15.3 3.8 %collective-permute-start.12 = (f32[128,1,1024]{2,1,0:T(1,128)}, f32[128,1,1024]{2,1,0:T(1,128)S(1)}, u32[]{:S(2)}, u32[]{:S(2)}) collective-permute-start(f32[128,1,1024]{2,1,0:T(1,128)} %collective-permute-done.8.refs_4_), channel_id=1, source_target_pairs={{0,1},{1,0},{2,3},{3,2},{4,5},{5,4},{6,7},{7,6},{8,9},{9,8},{10,11... | collective-permute-start | bytes 1572872 | tf_op jit(solution)/shard_map/ppermute | solution.py:202
  17.6 4.6 %collective-permute-start.15 = (f32[176,128]{1,0:T(8,128)S(1)}, f32[176,128]{1,0:T(8,128)S(1)}, u32[]{:S(2)}, u32[]{:S(2)}) collective-permute-start(f32[176,128]{1,0:T(8,128)S(1)} %collective-permute-done.13.refs_3_), channel_id=1, source_target_pairs={{0,4},{4,0},{8,12},{12,8},{16,20},{20,16},{24,28},{28,24},{1,5},{5... | collective-permute-start | bytes 270344 | tf_op jit(solution)/shard_map/ppermute | solution.py:202

commit v6 on v4

--- a/solution.py
+++ b/solution.py
@@ -122,12 +122,14 @@
 
 def order_kernel(depth, count, *refs):
     tasks_ref, meta_ref = refs[:2]
-    tiles, (out_ref, held, sem) = refs[2 : 2 + count], refs[2 + count :]
+    tiles, (base_ref, out_ref, rows_ref, held, sem, base_sem) = refs[2 : 2 + count], refs[2 + count :]
     own = lax.axis_index("vir")
     chosen = jnp.bitwise_xor(tasks_ref[own], own)
     copies = [pltpu.make_async_copy(tile_ref.at[:, 0, :], held, sem) for tile_ref in tiles]
     for number, copy in enumerate(copies):
         pl.when(chosen == number)(copy.start)
+    load = pltpu.make_async_copy(base_ref.at[:, 0, :], rows_ref, base_sem)
+    load.start()
     width, slots, size = meta_ref.shape[1], GROUP * depth, 3 * LANES
     starts = range(0, slots, size)
     places = [(iota((min(size, slots - at), width), 0) + at == meta_ref[:1]).astype(jnp.bfloat16) for at in starts]
@@ -135,27 +137,31 @@
     both = jnp.concatenate(split(held[...]), axis=0)
     for at, place in zip(starts, places):
         out_ref[:, at : at + place.shape[0]] = dot(both, place, NT).astype(jnp.bfloat16)
-
-
-def order(tasks, meta, tiles, depth):
+    load.wait()
+
+
+def order(tasks, meta, tiles, base, depth):
     height, _, width = tiles[0].shape
     smem, vmem = pl.BlockSpec(memory_space=pltpu.SMEM), pl.BlockSpec(memory_space=pltpu.VMEM)
     return pl.pallas_call(
         functools.partial(order_kernel, depth, len(tiles)),
-        out_shape=jax.ShapeDtypeStruct((2 * height, GROUP * depth), jnp.bfloat16),
-        in_specs=[smem, vmem] + [pl.BlockSpec(memory_space=pltpu.HBM)] * len(tiles),
-        out_specs=vmem,
-        scratch_shapes=[pltpu.VMEM((height, width), jnp.float32), pltpu.SemaphoreType.DMA],
+        out_shape=(
+            jax.ShapeDtypeStruct((2 * height, GROUP * depth), jnp.bfloat16),
+            jax.ShapeDtypeStruct((height, width), base.dtype),
+        ),
+        in_specs=[smem, vmem] + [pl.BlockSpec(memory_space=pltpu.HBM)] * len(tiles) + [pl.BlockSpec(memory_space=pl.ANY)],
+        out_specs=(vmem, vmem),
+        scratch_shapes=[pltpu.VMEM((height, width), jnp.float32), pltpu.SemaphoreType.DMA, pltpu.SemaphoreType.DMA],
         compiler_params=pltpu.CompilerParams(vmem_limit_bytes=32 << 20),
         cost_estimate=pl.CostEstimate(
             flops=40 * height * width * GROUP * depth, bytes_accessed=4 * height * width, transcendentals=0
         ),
         name="order_amplitudes",
-    )(tasks, meta, *tiles)
+    )(tasks, meta, *tiles, base)
 
 
 def ladder_kernel(depth, masks, count, meta_ref, amps_ref, *refs):
-    pieces, (base_ref, out_ref, held, load_sem, store_sem) = refs[:count], refs[count:]
+    pieces, (base_ref, out_ref, held, store_sem) = refs[:count], refs[count:]
     block = lax.axis_index("occ")
     height, width = held.shape
     size = pieces[0].shape[1]
@@ -164,31 +170,28 @@
         places = [pl.ds(0, size)]
     else:
         places = [pl.ds(pl.multiple_of(jnp.bitwise_xor(block, mask) * size, LANES), size) for mask in masks]
-    load = pltpu.make_async_copy(base_ref.at[:, 0, :], held, load_sem)
-    load.start()
     high, low = split(jnp.concatenate([piece[...] for piece in pieces], axis=1))
     irrep = jnp.concatenate([meta_ref[1:2, place] for place in places], axis=1)
     zero = jnp.zeros((), jnp.bfloat16)
     blocks = lambda values: jnp.concatenate([jnp.where(irrep == g, values, zero) for g in range(GROUP)], axis=0)
     both = dot(amps_ref[...], blocks(high), NN)
     ladder = both[:height] + both[height:] + dot(amps_ref[:height], blocks(low), NN)
-    load.wait()
     for n, place in enumerate(places):
-        held[:, place] += ladder[:, n * size : (n + 1) * size]
+        held[:, place] = base_ref[:, place] + ladder[:, n * size : (n + 1) * size]
     store = pltpu.make_async_copy(held, out_ref.at[:, 0, :], store_sem)
     store.start()
     store.wait()
 
 
 def ladder(meta, amps, masks, pieces, base, depth):
-    height, _, width = base.shape
+    height, width = base.shape
     vmem, hbm = pl.BlockSpec(memory_space=pltpu.VMEM), pl.BlockSpec(memory_space=pl.ANY)
     return pl.pallas_call(
         functools.partial(ladder_kernel, depth, masks, len(pieces)),
-        out_shape=jax.ShapeDtypeStruct(base.shape, base.dtype),
-        in_specs=[vmem, vmem] + [vmem] * len(pieces) + [hbm],
+        out_shape=jax.ShapeDtypeStruct((height, 1, width), base.dtype),
+        in_specs=[vmem, vmem] + [vmem] * len(pieces) + [vmem],
         out_specs=hbm,
-        scratch_shapes=[pltpu.VMEM((height, width), jnp.float32), pltpu.SemaphoreType.DMA, pltpu.SemaphoreType.DMA],
+        scratch_shapes=[pltpu.VMEM((height, width), jnp.float32), pltpu.SemaphoreType.DMA],
         compiler_params=pltpu.CompilerParams(vmem_limit_bytes=48 << 20),
         cost_estimate=pl.CostEstimate(
             flops=6 * height * width * GROUP * depth, bytes_accessed=8 * height * width, transcendentals=0
@@ -249,7 +252,7 @@
             tiles = {number: after(tile, direct) if number else tile for number, tile in tiles.items()}
             tiles = other_swaps(tiles, vir_size)
         tiles, base = lax.optimization_barrier((tiles, base))
-        ordered = order(tasks, meta, tiles, depth)
+        ordered, base = order(tasks, meta, tiles, base, depth)
         return ladder(meta, ordered, sum(blocks, ()), list(blocks.values()), base, depth)
 
     most = count(tasks, pair_tiles, irreps, width)

time: 25.1 us -> 24.7 us (0.984)
  waiting for transfers between devices: 3.93 us -> 3.56 us
    pallas_call x1, Pallas kernels: 2.68 us -> 2.29 us  [ladder(): pl.pallas_call(functools.partial(ladder_kernel, depth, masks, len(pieces)...]
    ppermute x9, waiting for transfers between devices: 3.93 us -> 3.56 us  [swap(): lax.ppermute(values, axis, [(device, device ^ mask) for device in range(s...]
    pallas_call x1, Pallas kernels: 2.29 us -> 2.65 us  [order(): pl.pallas_call(functools.partial(order_kernel, depth, len(tiles)), out_sh...]
  transfers between devices with their start and end apart: 9 -> 9, of which waited for: 4 -> 4; matrix products, arithmetic and copies ran while one was open for 0% -> 0% of each run, Pallas kernels for 20% -> 22%
where the time goes in v6:
time: 24.7 us; the launch traced here: 24.5 us
  starting transfers between devices  12.5 us (51%)
  Pallas kernels  7.56 us (31%)
  waiting for transfers between devices  3.56 us (14%)
  loops' own time  0.64 us (3%)
    ppermute x9, starting transfers between devices, swap(): lax.ppermute(values, axis, [(device, device ^ mask) for device in range(s...  12.5 us
    ppermute x9, waiting for transfers between devices, swap(): lax.ppermute(values, axis, [(device, device ^ mask) for device in range(s...  3.56 us
    pallas_call x1, Pallas kernels, order(): pl.pallas_call(functools.partial(order_kernel, depth, len(tiles)), out_sh...  2.65 us
    pallas_call x1, Pallas kernels, ladder(): pl.pallas_call(functools.partial(ladder_kernel, depth, masks, len(pieces)...  2.29 us
    pallas_call x1, Pallas kernels, count(): pl.pallas_call(functools.partial(count_kernel, width), out_shape=jax.Shap...  1.4 us
    pallas_call x1, Pallas kernels, prep(): pl.pallas_call(functools.partial(prep_kernel, depth), out_shape=(jax.Shap...  1.23 us
    another operation x1, loops' own time, shards(): lax.while_loop(lambda state: state[0][0] < most[0], lambda state: (state[...  0.64 us
  transfers between devices with their start and end apart: 9, of which 4 were waited for; matrix products, arithmetic and copies ran while one was open for 0% of the time, Pallas kernels for 22%

profile of v6, /device:TPU:0, one launch (start us, length us, event | category | flops | bytes accessed | tf_op | source)
XLA Modules:
  0.0 24.5 jit_solution(12672364241792092519)
XLA Ops:
  0.0 0.0 copy-start.4
  0.0 0.0 copy-start
  0.0 0.0 copy-start.1
  0.0 0.0 copy-start.3
  0.0 0.0 copy-start.5
  0.0 0.0 copy-start.2
  0.0 3.0 %collective-permute-start.8 = (f32[128,1,1024]{2,1,0:T(1,128)}, f32[128,1,1024]{2,1,0:T(1,128)}, u32[]{:S(2)}, u32[]{:S(2)}) collective-permute-start(f32[128,1,1024]{2,1,0:T(1,128)} %refs_2_), channel_id=1, source_target_pairs={{0,2},{1,3},{2,0},{3,1},{4,6},{5,7},{6,4},{7,5},{8,10},{9,11},{10,... | collective-permute-start | bytes 1572872 | tf_op jit(solution)/shard_map/ppermute | solution.py:204
  3.1 0.0 collective-permute-start.7
  3.1 0.0 copy-done.4
  3.1 0.1 copy.7.pairs_ref
  3.2 0.0 copy-done
  3.2 0.0 copy-done.1
  3.2 0.0 copy-done.3
  3.2 1.2 %compact.3 = (f32[176,128]{1,0:T(8,128)S(1)}, s32[8,1024]{1,0:T(8,128)S(1)}) custom-call(s32[1]{0:T(128)} %constant.6.clone.1.first_ref, s32[4]{0:T(128)S(1)} %copy-done.3, s32[4,2]{1,0:T(4,128)S(1)} %copy.7.pairs_ref, s32[19,32]{1,0:T(8,128)S(1)} %copy-done.1, f32[128,1024]{1,0:T(8,128)S(1)} %bitcast.3), custom_call_target="tpu_custom_call" | custom-call | flops 92274688 | bytes 524288 | tf_op jit(solution)/shard_map/compact/pallas_call | solution.py:87
  4.4 2.6 %collective-permute-start.9 = (f32[176,128]{1,0:T(8,128)S(1)}, f32[176,128]{1,0:T(8,128)S(1)}, u32[]{:S(2)}, u32[]{:S(2)}) collective-permute-start(f32[176,128]{1,0:T(8,128)S(1)} %get-tuple-element.105.refs_0_), channel_id=1, source_target_pairs={{0,16},{4,20},{8,24},{12,28},{16,0},{20,4},{24,8},{28,12},{1,17},{... | collective-permute-start | bytes 270344 | tf_op jit(solution)/shard_map/ppermute | solution.py:204
  7.1 1.6 %collective-permute-start.10 = (f32[176,128]{1,0:T(8,128)S(1)}, f32[176,128]{1,0:T(8,128)S(1)}, u32[]{:S(2)}, u32[]{:S(2)}) collective-permute-start(f32[176,128]{1,0:T(8,128)S(1)} %get-tuple-element.105.refs_0_), channel_id=1, source_target_pairs={{0,8},{4,12},{8,0},{12,4},{16,24},{20,28},{24,16},{28,20},{1,9},{5... | collective-permute-start | bytes 270344 | tf_op jit(solution)/shard_map/ppermute | solution.py:204
  8.6 1.4 %count.1 = s32[1]{0:T(128)} custom-call(s32[4]{0:T(128)S(1)} %copy-done.3, s32[4,2]{1,0:T(4,128)S(1)} %copy.7.pairs_ref, s32[19,32]{1,0:T(8,128)S(1)} %copy-done.1), custom_call_target="tpu_custom_call" | custom-call | tf_op jit(solution)/shard_map/count/pallas_call | solution.py:114
  10.0 1.6 %collective-permute-start.11 = (f32[176,128]{1,0:T(8,128)S(1)}, f32[176,128]{1,0:T(8,128)S(1)}, u32[]{:S(2)}, u32[]{:S(2)}) collective-permute-start(f32[176,128]{1,0:T(8,128)S(1)} %get-tuple-element.105.refs_0_), channel_id=1, source_target_pairs={{0,4},{4,0},{8,12},{12,8},{16,20},{20,16},{24,28},{28,24},{1,5},{5... | collective-permute-start | bytes 270344 | tf_op jit(solution)/shard_map/ppermute | solution.py:204
  11.6 0.8 %collective-permute-done.9.refs_1_ = f32[176,128]{1,0:T(8,128)S(1)} collective-permute-done((f32[176,128]{1,0:T(8,128)S(1)}, f32[176,128]{1,0:T(8,128)S(1)}, u32[]{:S(2)}, u32[]{:S(2)}) %collective-permute-start.9) | collective-permute-done | bytes 90144 | tf_op jit(solution)/shard_map/ppermute | solution.py:204
  12.4 0.6 %collective-permute-start.13 = (f32[176,128]{1,0:T(8,128)S(1)}, f32[176,128]{1,0:T(8,128)S(1)}, u32[]{:S(2)}, u32[]{:S(2)}) collective-permute-start(f32[176,128]{1,0:T(8,128)S(1)} %collective-permute-done.9.refs_1_), channel_id=1, source_target_pairs={{0,8},{4,12},{8,0},{12,4},{16,24},{20,28},{24,16},{28,20},{1,9},{5... | collective-permute-start | bytes 270344 | tf_op jit(solution)/shard_map/ppermute | solution.py:204
  13.0 0.0 collective-permute-done.10.refs_2_
  13.0 1.6 %collective-permute-start.14 = (f32[352,128]{1,0:T(8,128)S(1)}, f32[352,128]{1,0:T(8,128)S(1)}, u32[]{:S(2)}, u32[]{:S(2)}) collective-permute-start(f32[352,128]{1,0:T(8,128)S(1)} %pad_maximum_fusion.1), channel_id=1, source_target_pairs={{0,4},{4,0},{8,12},{12,8},{16,20},{20,16},{24,28},{28,24},{1,5},{5... | collective-permute-start | bytes 540680 | tf_op jit(solution)/shard_map/ppermute | solution.py:204
  14.6 0.0 collective-permute-done.11.refs_4_
  14.6 0.7 %collective-permute-done.8.refs_4_ = f32[128,1,1024]{2,1,0:T(1,128)} collective-permute-done((f32[128,1,1024]{2,1,0:T(1,128)}, f32[128,1,1024]{2,1,0:T(1,128)}, u32[]{:S(2)}, u32[]{:S(2)}) %collective-permute-start.8) | collective-permute-done | bytes 524320 | tf_op jit(solution)/shard_map/ppermute | solution.py:204
  15.3 0.0 collective-permute-start.12
  15.3 1.6 %collective-permute-done.13.refs_3_ = f32[176,128]{1,0:T(8,128)S(1)} collective-permute-done((f32[176,128]{1,0:T(8,128)S(1)}, f32[176,128]{1,0:T(8,128)S(1)}, u32[]{:S(2)}, u32[]{:S(2)}) %collective-permute-start.13) | collective-permute-done | bytes 90144 | tf_op jit(solution)/shard_map/ppermute | solution.py:204
  17.0 0.0 collective-permute-done.7.refs_3_
  17.0 0.0 copy-done.5
  17.0 0.0 copy-done.2
  17.0 0.6 %while.11 = (s32[1]{0:T(128)}, f32[128,1,1024]{2,1,0:T(1,128)S(1)}, s32[1]{0:T(128)}, s32[4]{0:T(128)S(1)}, s32[4,2]{1,0:T(4,128)S(1)}, /*index=5*/s32[19,32]{1,...) while((s32[1]{0:T(128)}, f32[128,1,1024]{2,1,0:T(1,128)S(1)}, ...), condition=%wide.region_1.0_spmd, body=%wide.region_0.0_spmd | while | flops 8581591040 | bytes 7078277 | solution.py:259
  17.6 1.6 %collective-permute-start.15 = (f32[176,128]{1,0:T(8,128)S(1)}, f32[176,128]{1,0:T(8,128)S(1)}, u32[]{:S(2)}, u32[]{:S(2)}) collective-permute-start(f32[176,128]{1,0:T(8,128)S(1)} %collective-permute-done.13.refs_3_), channel_id=1, source_target_pairs={{0,4},{4,0},{8,12},{12,8},{16,20},{20,16},{24,28},{28,24},{1,5},{5... | collective-permute-start | bytes 270344 | tf_op jit(solution)/shard_map/ppermute | solution.py:204
  19.2 0.0 collective-permute-done.12.refs_5_
  19.2 2.7 %order_amplitudes.3 = (bf16[256,1408]{1,0:T(8,128)(2,1)S(1)}, f32[128,1024]{1,0:T(8,128)S(1)}) custom-call(s32[4]{0:T(128)S(1)} %get-tuple-element.266, s32[8,1024]{1,0:T(8,128)S(1)} %get-tuple-element.104.refs_1_.meta_ref, f32[128,1,1024]{2,1,0:T(1,128)S(1)} %get-tuple-element.269, f32[128,1,1024]{2,1,0:T(1,128)S(1)} %get-tuple-element.271, ...), custom_call_target="tpu_custom_call" | custom-call | flops 7381975040 | bytes 524288 | tf_op jit(solution)/shard_map/order_amplitudes/pallas_call | solution.py:146
  21.9 0.0 collective-permute-done.14.refs_5_
  21.9 0.4 %collective-permute-done.15.refs_6_ = f32[176,128]{1,0:T(8,128)S(1)} collective-permute-done((f32[176,128]{1,0:T(8,128)S(1)}, f32[176,128]{1,0:T(8,128)S(1)}, u32[]{:S(2)}, u32[]{:S(2)}) %collective-permute-start.15) | collective-permute-done | bytes 90144 | tf_op jit(solution)/shard_map/ppermute | solution.py:204
  22.2 2.3 %ladder.3 = f32[128,1,1024]{2,1,0:T(1,128)} custom-call(s32[8,1024]{1,0:T(8,128)S(1)} %get-tuple-element.104.refs_1_.meta_ref, bf16[256,1408]{1,0:T(8,128)(2,1)S(1)} %get-tuple-element.113.amps_ref, f32[176,128]{1,0:T(8,128)S(1)} %get-tuple-element.105.refs_0_, f32[176,128]{1,0:T(8,128)S(1)} %collective-permute-done.9.refs_1_, ...), custom_call_target="tpu_custom_call" | custom-call | flops 1107296256 | bytes 1048576 | tf_op jit(solution)/shard_map/ladder/pallas_call | solution.py:189
  (1 shorter events, 0.0 us)
Async XLA Ops:
  0.0 3.1 %copy-start.4 = (s32[4,2]{0,1:T(2,128)S(1)}, s32[4,2]{0,1:T(2,128)}, u32[]{:S(2)}) copy-start(s32[4,2]{0,1:T(2,128)} %param.12) | copy-start | bytes 100
  0.0 3.2 %copy-start = (f32[1,128,1024]{2,1,0:T(8,128)S(1)}, f32[1,128,1024]{2,1,0:T(8,128)}, u32[]{:S(2)}) copy-start(f32[1,128,1024]{2,1,0:T(8,128)} %param.10) | copy-start | bytes 1572868
  0.0 3.2 %copy-start.1 = (s32[19,32]{1,0:T(8,128)S(1)}, s32[19,32]{1,0:T(8,128)}, u32[]{:S(2)}) copy-start(s32[19,32]{1,0:T(8,128)} %irreps_ref.3) | copy-start | bytes 7300
  0.0 3.2 %copy-start.3 = (s32[4]{0:T(128)S(1)}, s32[4]{0:T(128)}, u32[]{:S(2)}) copy-start(s32[4]{0:T(128)} %refs_0_.1) | copy-start | bytes 52
  0.0 17.0 %copy-start.5 = (f32[128,1,1024]{2,1,0:T(1,128)S(1)}, f32[128,1,1024]{2,1,0:T(1,128)}, u32[]{:S(2)}) copy-start(f32[128,1,1024]{2,1,0:T(1,128)} %refs_2_) | copy-start | bytes 1572868
  0.0 17.0 %copy-start.2 = (f32[128,1,1024]{2,1,0:T(1,128)S(1)}, f32[128,1,1024]{2,1,0:T(1,128)}, u32[]{:S(2)}) copy-start(f32[128,1,1024]{2,1,0:T(1,128)} %param.9) | copy-start | bytes 1572868
  0.0 15.3 %collective-permute-start.8 = (f32[128,1,1024]{2,1,0:T(1,128)}, f32[128,1,1024]{2,1,0:T(1,128)}, u32[]{:S(2)}, u32[]{:S(2)}) collective-permute-start(f32[128,1,1024]{2,1,0:T(1,128)} %refs_2_), channel_id=1, source_target_pairs={{0,2},{1,3},{2,0},{3,1},{4,6},{5,7},{6,4},{7,5},{8,10},{9,11},{10,... | collective-permute-start | bytes 1572872 | tf_op jit(solution)/shard_map/ppermute | solution.py:204
  3.1 13.9 %collective-permute-start.7 = (f32[128,1,1024]{2,1,0:T(1,128)}, f32[128,1,1024]{2,1,0:T(1,128)S(1)}, u32[]{:S(2)}, u32[]{:S(2)}) collective-permute-start(f32[128,1,1024]{2,1,0:T(1,128)} %refs_2_), channel_id=1, source_target_pairs={{0,1},{1,0},{2,3},{3,2},{4,5},{5,4},{6,7},{7,6},{8,9},{9,8},{10,11... | collective-permute-start | bytes 1572872 | tf_op jit(solution)/shard_map/ppermute | solution.py:204
  4.4 8.0 %collective-permute-start.9 = (f32[176,128]{1,0:T(8,128)S(1)}, f32[176,128]{1,0:T(8,128)S(1)}, u32[]{:S(2)}, u32[]{:S(2)}) collective-permute-start(f32[176,128]{1,0:T(8,128)S(1)} %get-tuple-element.105.refs_0_), channel_id=1, source_target_pairs={{0,16},{4,20},{8,24},{12,28},{16,0},{20,4},{24,8},{28,12},{1,17},{... | collective-permute-start | bytes 270344 | tf_op jit(solution)/shard_map/ppermute | solution.py:204
  7.1 6.0 %collective-permute-start.10 = (f32[176,128]{1,0:T(8,128)S(1)}, f32[176,128]{1,0:T(8,128)S(1)}, u32[]{:S(2)}, u32[]{:S(2)}) collective-permute-start(f32[176,128]{1,0:T(8,128)S(1)} %get-tuple-element.105.refs_0_), channel_id=1, source_target_pairs={{0,8},{4,12},{8,0},{12,4},{16,24},{20,28},{24,16},{28,20},{1,9},{5... | collective-permute-start | bytes 270344 | tf_op jit(solution)/shard_map/ppermute | solution.py:204
  10.0 4.6 %collective-permute-start.11 = (f32[176,128]{1,0:T(8,128)S(1)}, f32[176,128]{1,0:T(8,128)S(1)}, u32[]{:S(2)}, u32[]{:S(2)}) collective-permute-start(f32[176,128]{1,0:T(8,128)S(1)} %get-tuple-element.105.refs_0_), channel_id=1, source_target_pairs={{0,4},{4,0},{8,12},{12,8},{16,20},{20,16},{24,28},{28,24},{1,5},{5... | collective-permute-start | bytes 270344 | tf_op jit(solution)/shard_map/ppermute | solution.py:204
  12.4 4.5 %collective-permute-start.13 = (f32[176,128]{1,0:T(8,128)S(1)}, f32[176,128]{1,0:T(8,128)S(1)}, u32[]{:S(2)}, u32[]{:S(2)}) collective-permute-start(f32[176,128]{1,0:T(8,128)S(1)} %collective-permute-done.9.refs_1_), channel_id=1, source_target_pairs={{0,8},{4,12},{8,0},{12,4},{16,24},{20,28},{24,16},{28,20},{1,9},{5... | collective-permute-start | bytes 270344 | tf_op jit(solution)/shard_map/ppermute | solution.py:204
  13.0 8.8 %collective-permute-start.14 = (f32[352,128]{1,0:T(8,128)S(1)}, f32[352,128]{1,0:T(8,128)S(1)}, u32[]{:S(2)}, u32[]{:S(2)}) collective-permute-start(f32[352,128]{1,0:T(8,128)S(1)} %pad_maximum_fusion.1), channel_id=1, source_target_pairs={{0,4},{4,0},{8,12},{12,8},{16,20},{20,16},{24,28},{28,24},{1,5},{5... | collective-permute-start | bytes 540680 | tf_op jit(solution)/shard_map/ppermute | solution.py:204
  15.3 3.9 %collective-permute-start.12 = (f32[128,1,1024]{2,1,0:T(1,128)}, f32[128,1,1024]{2,1,0:T(1,128)S(1)}, u32[]{:S(2)}, u32[]{:S(2)}) collective-permute-start(f32[128,1,1024]{2,1,0:T(1,128)} %collective-permute-done.8.refs_4_), channel_id=1, source_target_pairs={{0,1},{1,0},{2,3},{3,2},{4,5},{5,4},{6,7},{7,6},{8,9},{9,8},{10,11... | collective-permute-start | bytes 1572872 | tf_op jit(solution)/shard_map/ppermute | solution.py:204
  17.6 4.6 %collective-permute-start.15 = (f32[176,128]{1,0:T(8,128)S(1)}, f32[176,128]{1,0:T(8,128)S(1)}, u32[]{:S(2)}, u32[]{:S(2)}) collective-permute-start(f32[176,128]{1,0:T(8,128)S(1)} %collective-permute-done.13.refs_3_), channel_id=1, source_target_pairs={{0,4},{4,0},{8,12},{12,8},{16,20},{20,16},{24,28},{28,24},{1,5},{5... | collective-permute-start | bytes 270344 | tf_op jit(solution)/shard_map/ppermute | solution.py:204

commit v7 on v6

--- a/solution.py
+++ b/solution.py
@@ -78,7 +78,8 @@
     live = jnp.bitwise_xor(outer, inner) == cd_irrep[:1]
     high, low = split(jnp.where(live, ints_ref[...], 0.0))
     pick = (iota((depth, width), 0) == rank).astype(jnp.bfloat16)
-    buf_ref[...] = dot(pick, high, NT) + dot(pick, low, NT)
+    both = dot(pick, jnp.concatenate([high, low], axis=0), NT)
+    buf_ref[...] = both[:, :height] + both[:, height:]
 
 
 def prep(first, tasks, pairs, irreps, ints, depth):

time: 24.7 us -> 24.6 us (level)
  no operation moved by 1% of the time
where the time goes in v7:
time: 24.6 us; the launch traced here: 24.4 us
  starting transfers between devices  12.5 us (51%)
  Pallas kernels  7.57 us (31%)
  waiting for transfers between devices  3.49 us (14%)
  loops' own time  0.64 us (3%)
    ppermute x9, starting transfers between devices, swap(): lax.ppermute(values, axis, [(device, device ^ mask) for device in range(s...  12.5 us
    ppermute x9, waiting for transfers between devices, swap(): lax.ppermute(values, axis, [(device, device ^ mask) for device in range(s...  3.49 us
    pallas_call x1, Pallas kernels, order(): pl.pallas_call(functools.partial(order_kernel, depth, len(tiles)), out_sh...  2.74 us
    pallas_call x1, Pallas kernels, ladder(): pl.pallas_call(functools.partial(ladder_kernel, depth, masks, len(pieces)...  2.29 us
    pallas_call x1, Pallas kernels, count(): pl.pallas_call(functools.partial(count_kernel, width), out_shape=jax.Shap...  1.4 us
    pallas_call x1, Pallas kernels, prep(): pl.pallas_call(functools.partial(prep_kernel, depth), out_shape=(jax.Shap...  1.15 us
    another operation x1, loops' own time, shards(): lax.while_loop(lambda state: state[0][0] < most[0], lambda state: (state[...  0.64 us
  transfers between devices with their start and end apart: 9, of which 4 were waited for; matrix products, arithmetic and copies ran while one was open for 0% of the time, Pallas kernels for 22%

profile of v7, /device:TPU:0, one launch (start us, length us, event | category | flops | bytes accessed | tf_op | source)
XLA Modules:
  0.0 24.4 jit_solution(5096491121983627559)
XLA Ops:
  0.0 0.0 copy-start.4
  0.0 0.0 copy-start
  0.0 0.0 copy-start.1
  0.0 0.0 copy-start.3
  0.0 0.0 copy-start.5
  0.0 0.0 copy-start.2
  0.0 3.0 %collective-permute-start.8 = (f32[128,1,1024]{2,1,0:T(1,128)}, f32[128,1,1024]{2,1,0:T(1,128)}, u32[]{:S(2)}, u32[]{:S(2)}) collective-permute-start(f32[128,1,1024]{2,1,0:T(1,128)} %refs_2_), channel_id=1, source_target_pairs={{0,2},{1,3},{2,0},{3,1},{4,6},{5,7},{6,4},{7,5},{8,10},{9,11},{10,... | collective-permute-start | bytes 1572872 | tf_op jit(solution)/shard_map/ppermute | solution.py:205
  3.1 0.0 collective-permute-start.7
  3.1 0.0 copy-done.4
  3.1 0.1 copy.7.pairs_ref
  3.2 0.0 copy-done
  3.2 0.0 copy-done.1
  3.2 0.0 copy-done.3
  3.2 1.1 %compact.3 = (f32[176,128]{1,0:T(8,128)S(1)}, s32[8,1024]{1,0:T(8,128)S(1)}) custom-call(s32[1]{0:T(128)} %constant.6.clone.1.first_ref, s32[4]{0:T(128)S(1)} %copy-done.3, s32[4,2]{1,0:T(4,128)S(1)} %copy.7.pairs_ref, s32[19,32]{1,0:T(8,128)S(1)} %copy-done.1, f32[128,1024]{1,0:T(8,128)S(1)} %bitcast.3), custom_call_target="tpu_custom_call" | custom-call | flops 92274688 | bytes 524288 | tf_op jit(solution)/shard_map/compact/pallas_call | solution.py:88
  4.3 2.7 %collective-permute-start.9 = (f32[176,128]{1,0:T(8,128)S(1)}, f32[176,128]{1,0:T(8,128)S(1)}, u32[]{:S(2)}, u32[]{:S(2)}) collective-permute-start(f32[176,128]{1,0:T(8,128)S(1)} %get-tuple-element.105.refs_0_), channel_id=1, source_target_pairs={{0,16},{4,20},{8,24},{12,28},{16,0},{20,4},{24,8},{28,12},{1,17},{... | collective-permute-start | bytes 270344 | tf_op jit(solution)/shard_map/ppermute | solution.py:205
  7.0 1.6 %collective-permute-start.10 = (f32[176,128]{1,0:T(8,128)S(1)}, f32[176,128]{1,0:T(8,128)S(1)}, u32[]{:S(2)}, u32[]{:S(2)}) collective-permute-start(f32[176,128]{1,0:T(8,128)S(1)} %get-tuple-element.105.refs_0_), channel_id=1, source_target_pairs={{0,8},{4,12},{8,0},{12,4},{16,24},{20,28},{24,16},{28,20},{1,9},{5... | collective-permute-start | bytes 270344 | tf_op jit(solution)/shard_map/ppermute | solution.py:205
  8.6 1.4 %count.1 = s32[1]{0:T(128)} custom-call(s32[4]{0:T(128)S(1)} %copy-done.3, s32[4,2]{1,0:T(4,128)S(1)} %copy.7.pairs_ref, s32[19,32]{1,0:T(8,128)S(1)} %copy-done.1), custom_call_target="tpu_custom_call" | custom-call | tf_op jit(solution)/shard_map/count/pallas_call | solution.py:115
  10.0 1.6 %collective-permute-start.11 = (f32[176,128]{1,0:T(8,128)S(1)}, f32[176,128]{1,0:T(8,128)S(1)}, u32[]{:S(2)}, u32[]{:S(2)}) collective-permute-start(f32[176,128]{1,0:T(8,128)S(1)} %get-tuple-element.105.refs_0_), channel_id=1, source_target_pairs={{0,4},{4,0},{8,12},{12,8},{16,20},{20,16},{24,28},{28,24},{1,5},{5... | collective-permute-start | bytes 270344 | tf_op jit(solution)/shard_map/ppermute | solution.py:205
  11.5 0.8 %collective-permute-done.9.refs_1_ = f32[176,128]{1,0:T(8,128)S(1)} collective-permute-done((f32[176,128]{1,0:T(8,128)S(1)}, f32[176,128]{1,0:T(8,128)S(1)}, u32[]{:S(2)}, u32[]{:S(2)}) %collective-permute-start.9) | collective-permute-done | bytes 90144 | tf_op jit(solution)/shard_map/ppermute | solution.py:205
  12.4 0.6 %collective-permute-start.13 = (f32[176,128]{1,0:T(8,128)S(1)}, f32[176,128]{1,0:T(8,128)S(1)}, u32[]{:S(2)}, u32[]{:S(2)}) collective-permute-start(f32[176,128]{1,0:T(8,128)S(1)} %collective-permute-done.9.refs_1_), channel_id=1, source_target_pairs={{0,8},{4,12},{8,0},{12,4},{16,24},{20,28},{24,16},{28,20},{1,9},{5... | collective-permute-start | bytes 270344 | tf_op jit(solution)/shard_map/ppermute | solution.py:205
  13.0 0.0 collective-permute-done.10.refs_2_
  13.0 1.6 %collective-permute-start.14 = (f32[352,128]{1,0:T(8,128)S(1)}, f32[352,128]{1,0:T(8,128)S(1)}, u32[]{:S(2)}, u32[]{:S(2)}) collective-permute-start(f32[352,128]{1,0:T(8,128)S(1)} %pad_maximum_fusion.1), channel_id=1, source_target_pairs={{0,4},{4,0},{8,12},{12,8},{16,20},{20,16},{24,28},{28,24},{1,5},{5... | collective-permute-start | bytes 540680 | tf_op jit(solution)/shard_map/ppermute | solution.py:205
  14.5 0.0 collective-permute-done.11.refs_4_
  14.6 0.7 %collective-permute-done.8.refs_4_ = f32[128,1,1024]{2,1,0:T(1,128)} collective-permute-done((f32[128,1,1024]{2,1,0:T(1,128)}, f32[128,1,1024]{2,1,0:T(1,128)}, u32[]{:S(2)}, u32[]{:S(2)}) %collective-permute-start.8) | collective-permute-done | bytes 524320 | tf_op jit(solution)/shard_map/ppermute | solution.py:205
  15.3 0.0 collective-permute-start.12
  15.3 1.6 %collective-permute-done.13.refs_3_ = f32[176,128]{1,0:T(8,128)S(1)} collective-permute-done((f32[176,128]{1,0:T(8,128)S(1)}, f32[176,128]{1,0:T(8,128)S(1)}, u32[]{:S(2)}, u32[]{:S(2)}) %collective-permute-start.13) | collective-permute-done | bytes 90144 | tf_op jit(solution)/shard_map/ppermute | solution.py:205
  16.9 0.0 collective-permute-done.7.refs_3_
  16.9 0.0 copy-done.5
  16.9 0.0 copy-done.2
  16.9 0.6 %while.11 = (s32[1]{0:T(128)}, f32[128,1,1024]{2,1,0:T(1,128)S(1)}, s32[1]{0:T(128)}, s32[4]{0:T(128)S(1)}, s32[4,2]{1,0:T(4,128)S(1)}, /*index=5*/s32[19,32]{1,...) while((s32[1]{0:T(128)}, f32[128,1,1024]{2,1,0:T(1,128)S(1)}, ...), condition=%wide.region_1.0_spmd, body=%wide.region_0.0_spmd | while | flops 8581591040 | bytes 7078277 | solution.py:260
  17.6 1.6 %collective-permute-start.15 = (f32[176,128]{1,0:T(8,128)S(1)}, f32[176,128]{1,0:T(8,128)S(1)}, u32[]{:S(2)}, u32[]{:S(2)}) collective-permute-start(f32[176,128]{1,0:T(8,128)S(1)} %collective-permute-done.13.refs_3_), channel_id=1, source_target_pairs={{0,4},{4,0},{8,12},{12,8},{16,20},{20,16},{24,28},{28,24},{1,5},{5... | collective-permute-start | bytes 270344 | tf_op jit(solution)/shard_map/ppermute | solution.py:205
  19.1 0.0 collective-permute-done.12.refs_5_
  19.1 2.7 %order_amplitudes.3 = (bf16[256,1408]{1,0:T(8,128)(2,1)S(1)}, f32[128,1024]{1,0:T(8,128)S(1)}) custom-call(s32[4]{0:T(128)S(1)} %get-tuple-element.266, s32[8,1024]{1,0:T(8,128)S(1)} %get-tuple-element.104.refs_1_.meta_ref, f32[128,1,1024]{2,1,0:T(1,128)S(1)} %get-tuple-element.269, f32[128,1,1024]{2,1,0:T(1,128)S(1)} %get-tuple-element.271, ...), custom_call_target="tpu_custom_call" | custom-call | flops 7381975040 | bytes 524288 | tf_op jit(solution)/shard_map/order_amplitudes/pallas_call | solution.py:147
  21.9 0.0 collective-permute-done.14.refs_5_
  21.9 0.3 %collective-permute-done.15.refs_6_ = f32[176,128]{1,0:T(8,128)S(1)} collective-permute-done((f32[176,128]{1,0:T(8,128)S(1)}, f32[176,128]{1,0:T(8,128)S(1)}, u32[]{:S(2)}, u32[]{:S(2)}) %collective-permute-start.15) | collective-permute-done | bytes 90144 | tf_op jit(solution)/shard_map/ppermute | solution.py:205
  22.2 2.3 %ladder.3 = f32[128,1,1024]{2,1,0:T(1,128)} custom-call(s32[8,1024]{1,0:T(8,128)S(1)} %get-tuple-element.104.refs_1_.meta_ref, bf16[256,1408]{1,0:T(8,128)(2,1)S(1)} %get-tuple-element.113.amps_ref, f32[176,128]{1,0:T(8,128)S(1)} %get-tuple-element.105.refs_0_, f32[176,128]{1,0:T(8,128)S(1)} %collective-permute-done.9.refs_1_, ...), custom_call_target="tpu_custom_call" | custom-call | flops 1107296256 | bytes 1048576 | tf_op jit(solution)/shard_map/ladder/pallas_call | solution.py:190
  (1 shorter events, 0.0 us)
Async XLA Ops:
  0.0 3.1 %copy-start.4 = (s32[4,2]{0,1:T(2,128)S(1)}, s32[4,2]{0,1:T(2,128)}, u32[]{:S(2)}) copy-start(s32[4,2]{0,1:T(2,128)} %param.12) | copy-start | bytes 100
  0.0 3.2 %copy-start = (f32[1,128,1024]{2,1,0:T(8,128)S(1)}, f32[1,128,1024]{2,1,0:T(8,128)}, u32[]{:S(2)}) copy-start(f32[1,128,1024]{2,1,0:T(8,128)} %param.10) | copy-start | bytes 1572868
  0.0 3.2 %copy-start.1 = (s32[19,32]{1,0:T(8,128)S(1)}, s32[19,32]{1,0:T(8,128)}, u32[]{:S(2)}) copy-start(s32[19,32]{1,0:T(8,128)} %irreps_ref.3) | copy-start | bytes 7300
  0.0 3.2 %copy-start.3 = (s32[4]{0:T(128)S(1)}, s32[4]{0:T(128)}, u32[]{:S(2)}) copy-start(s32[4]{0:T(128)} %refs_0_.1) | copy-start | bytes 52
  0.0 16.9 %copy-start.5 = (f32[128,1,1024]{2,1,0:T(1,128)S(1)}, f32[128,1,1024]{2,1,0:T(1,128)}, u32[]{:S(2)}) copy-start(f32[128,1,1024]{2,1,0:T(1,128)} %refs_2_) | copy-start | bytes 1572868
  0.0 16.9 %copy-start.2 = (f32[128,1,1024]{2,1,0:T(1,128)S(1)}, f32[128,1,1024]{2,1,0:T(1,128)}, u32[]{:S(2)}) copy-start(f32[128,1,1024]{2,1,0:T(1,128)} %param.9) | copy-start | bytes 1572868
  0.0 15.3 %collective-permute-start.8 = (f32[128,1,1024]{2,1,0:T(1,128)}, f32[128,1,1024]{2,1,0:T(1,128)}, u32[]{:S(2)}, u32[]{:S(2)}) collective-permute-start(f32[128,1,1024]{2,1,0:T(1,128)} %refs_2_), channel_id=1, source_target_pairs={{0,2},{1,3},{2,0},{3,1},{4,6},{5,7},{6,4},{7,5},{8,10},{9,11},{10,... | collective-permute-start | bytes 1572872 | tf_op jit(solution)/shard_map/ppermute | solution.py:205
  3.1 13.8 %collective-permute-start.7 = (f32[128,1,1024]{2,1,0:T(1,128)}, f32[128,1,1024]{2,1,0:T(1,128)S(1)}, u32[]{:S(2)}, u32[]{:S(2)}) collective-permute-start(f32[128,1,1024]{2,1,0:T(1,128)} %refs_2_), channel_id=1, source_target_pairs={{0,1},{1,0},{2,3},{3,2},{4,5},{5,4},{6,7},{7,6},{8,9},{9,8},{10,11... | collective-permute-start | bytes 1572872 | tf_op jit(solution)/shard_map/ppermute | solution.py:205
  4.3 8.0 %collective-permute-start.9 = (f32[176,128]{1,0:T(8,128)S(1)}, f32[176,128]{1,0:T(8,128)S(1)}, u32[]{:S(2)}, u32[]{:S(2)}) collective-permute-start(f32[176,128]{1,0:T(8,128)S(1)} %get-tuple-element.105.refs_0_), channel_id=1, source_target_pairs={{0,16},{4,20},{8,24},{12,28},{16,0},{20,4},{24,8},{28,12},{1,17},{... | collective-permute-start | bytes 270344 | tf_op jit(solution)/shard_map/ppermute | solution.py:205
  7.0 6.0 %collective-permute-start.10 = (f32[176,128]{1,0:T(8,128)S(1)}, f32[176,128]{1,0:T(8,128)S(1)}, u32[]{:S(2)}, u32[]{:S(2)}) collective-permute-start(f32[176,128]{1,0:T(8,128)S(1)} %get-tuple-element.105.refs_0_), channel_id=1, source_target_pairs={{0,8},{4,12},{8,0},{12,4},{16,24},{20,28},{24,16},{28,20},{1,9},{5... | collective-permute-start | bytes 270344 | tf_op jit(solution)/shard_map/ppermute | solution.py:205
  10.0 4.6 %collective-permute-start.11 = (f32[176,128]{1,0:T(8,128)S(1)}, f32[176,128]{1,0:T(8,128)S(1)}, u32[]{:S(2)}, u32[]{:S(2)}) collective-permute-start(f32[176,128]{1,0:T(8,128)S(1)} %get-tuple-element.105.refs_0_), channel_id=1, source_target_pairs={{0,4},{4,0},{8,12},{12,8},{16,20},{20,16},{24,28},{28,24},{1,5},{5... | collective-permute-start | bytes 270344 | tf_op jit(solution)/shard_map/ppermute | solution.py:205
  12.4 4.5 %collective-permute-start.13 = (f32[176,128]{1,0:T(8,128)S(1)}, f32[176,128]{1,0:T(8,128)S(1)}, u32[]{:S(2)}, u32[]{:S(2)}) collective-permute-start(f32[176,128]{1,0:T(8,128)S(1)} %collective-permute-done.9.refs_1_), channel_id=1, source_target_pairs={{0,8},{4,12},{8,0},{12,4},{16,24},{20,28},{24,16},{28,20},{1,9},{5... | collective-permute-start | bytes 270344 | tf_op jit(solution)/shard_map/ppermute | solution.py:205
  13.0 8.9 %collective-permute-start.14 = (f32[352,128]{1,0:T(8,128)S(1)}, f32[352,128]{1,0:T(8,128)S(1)}, u32[]{:S(2)}, u32[]{:S(2)}) collective-permute-start(f32[352,128]{1,0:T(8,128)S(1)} %pad_maximum_fusion.1), channel_id=1, source_target_pairs={{0,4},{4,0},{8,12},{12,8},{16,20},{20,16},{24,28},{28,24},{1,5},{5... | collective-permute-start | bytes 540680 | tf_op jit(solution)/shard_map/ppermute | solution.py:205
  15.3 3.8 %collective-permute-start.12 = (f32[128,1,1024]{2,1,0:T(1,128)}, f32[128,1,1024]{2,1,0:T(1,128)S(1)}, u32[]{:S(2)}, u32[]{:S(2)}) collective-permute-start(f32[128,1,1024]{2,1,0:T(1,128)} %collective-permute-done.8.refs_4_), channel_id=1, source_target_pairs={{0,1},{1,0},{2,3},{3,2},{4,5},{5,4},{6,7},{7,6},{8,9},{9,8},{10,11... | collective-permute-start | bytes 1572872 | tf_op jit(solution)/shard_map/ppermute | solution.py:205
  17.6 4.6 %collective-permute-start.15 = (f32[176,128]{1,0:T(8,128)S(1)}, f32[176,128]{1,0:T(8,128)S(1)}, u32[]{:S(2)}, u32[]{:S(2)}) collective-permute-start(f32[176,128]{1,0:T(8,128)S(1)} %collective-permute-done.13.refs_3_), channel_id=1, source_target_pairs={{0,4},{4,0},{8,12},{12,8},{16,20},{20,16},{24,28},{28,24},{1,5},{5... | collective-permute-start | bytes 270344 | tf_op jit(solution)/shard_map/ppermute | solution.py:205
